TPU v7x, 128 devices: a whole 4x4x4 slice. The times are simulated.
128 devices in a mesh: integral: 8 (over x, core), pair: 16 (over y, z).
Axes of the slice: x: 4, y: 4, z: 4, core: 2. Of those that a mesh axis runs over, the one named last changes fastest.
Arguments:
- t2_tiles: bfloat16 [2048, 40, 1024], P('pair', None, 'integral'), may hold values from -6 to 6
- keep_tile: int32 [40], replicated, may hold values from 0 to 63, as said below
- integrals: bfloat16 [64, 1024, 8192], P('pair', None, 'integral'), may hold values from -0.0625 to 0.0625
Outputs:
- residual: bfloat16 [2048, 8192], P('pair', 'integral')
Inputs may be any that keep to these rules, and one draw needn't show every extreme that they name: `keep_tile`: 40 distinct tile numbers in no particular order; tile k lies in the integral rows of pair index k // 4; at least one pair index has all 4 of its tiles listed.
All inputs are finite; a program needn't handle non-finite values.
Results may differ from a plain program's by a relative error of at most 0.0014.
Values may be sent and summed in bfloat16 or wider, within the bound.
No kernel may reach another device: no remote copies, remote signals or barrier semaphores. Data moves between devices by JAX's collectives and lax.ppermute only.
A program may use at most 128 MiB of HBM per device.

v0:
```python
import jax
import jax.numpy as jnp
from jax import lax
from jax.sharding import PartitionSpec as P


def on_device(t2_tiles, keep_tile, integrals):
    pair_count = lax.axis_size("pair")
    myself = lax.axis_index("pair")
    op_dev = t2_tiles.shape[0]
    kept_count = t2_tiles.shape[1]
    slot_count = integrals.shape[0]
    owners = keep_tile // slot_count
    positions = jnp.arange(kept_count, dtype=jnp.int32)
    earlier = (positions[None, :] < positions[:, None]) & (owners[None, :] == owners[:, None])
    ranking = jnp.sum(earlier.astype(jnp.int32), axis=1)
    matches = (ranking[:, None, None] == jnp.arange(slot_count, dtype=jnp.int32)[None, :, None]) & (
        owners[:, None, None] == jnp.arange(pair_count, dtype=jnp.int32)[None, None, :]
    )
    match_ints = matches.astype(jnp.int32)
    filled = jnp.sum(match_ints, axis=0)
    where_at = jnp.sum(match_ints * positions[:, None, None], axis=0)
    outgoing = jnp.take(t2_tiles, where_at.reshape(-1), axis=1)
    outgoing = outgoing.reshape(op_dev, slot_count, pair_count, t2_tiles.shape[2])
    outgoing = outgoing * filled.astype(jnp.bfloat16)[None, :, :, None]
    received = lax.all_to_all(outgoing, "pair", split_axis=2, concat_axis=0, tiled=True)
    received = received.reshape(received.shape[0], slot_count, t2_tiles.shape[2])
    my_slots = lax.dynamic_index_in_dim(where_at, myself, 1, keepdims=False)
    my_filled = lax.dynamic_index_in_dim(filled, myself, 1, keepdims=False)
    local_tile = jnp.where(my_filled > 0, jnp.take(keep_tile, my_slots) - myself * slot_count, 0)
    contract = (((1, 2), (0, 1)), ((), ()))
    chosen = jnp.take(integrals, local_tile, axis=0)
    partial_value = lax.dot_general(
        lax.all_gather(received, "integral", axis=2, tiled=True),
        chosen,
        contract,
        preferred_element_type=jnp.float32,
    )
    my_rows = lax.psum_scatter(partial_value, "pair", scatter_dimension=0, tiled=True)
    return (0.5 * my_rows).astype(jnp.bfloat16)


def solution(mesh):
    placed = (P("pair", None, "integral"), P(), P("pair", None, "integral"))
    return jax.shard_map(
        on_device, mesh=mesh, in_specs=placed, out_specs=P("pair", "integral"), check_vma=False
    )
```

profile of v0, /device:TPU:0, one launch (start us, length us, event | category | flops | bytes accessed | tf_op | source)
XLA Modules:
  0.0 266.3 jit_solution(729889983576818680)
XLA Ops:
  6.5 0.0 copy-start
  6.5 0.0 all-gather.2.cloned.1.call-start
  6.5 0.8 and_select_fusion.1
  7.3 0.2 convert_reduce_fusion
  7.5 0.2 fusion.8
  7.8 0.1 reshape.105
  7.8 0.1 copy.20
  7.9 0.1 copy.22
  8.0 0.0 copy-done
  8.0 8.7 %gather_fusion = bf16[64,128,128]{2,0,1:T(8,128)(2,1)S(1)} fusion(bf16[128,40,128]{2,1,0:T(8,128)(2,1)S(1)} %copy-done, s32[1024]{0:T(1024)S(1)} %pad_clamp_fusion.2), kind=kCustom, calls=%fused_computation | custom fusion | bytes 4194560 | tf_op jit(solution)/shard_map/jit(_take)/gather | solution.py:23
  16.8 3.6 %fusion.6 = bf16[128,4,16,128]{3,0,1,2:T(8,128)(2,1)S(1)} fusion(bf16[128,4,16,128]{3,2,1,0:T(8,128)(2,1)S(1)} %bitcast.15, pred[4,16]{0,1:T(8,128)(4,1)S(1)} %copy.20, bf16[4,16]{0,1:T(8,128)(2,1)S(1)} %copy.22), kind=kLoop, calls=%fused_computation.12 | loop fusion | flops 2097152 | bytes 4194496 | tf_op jit(solution)/shard_map/mul | solution.py:25
  20.4 36.2 %all_to_all.15 = bf16[128,4,16,128]{3,0,1,2:T(8,128)(2,1)S(1)} all-to-all(bf16[128,4,16,128]{3,0,1,2:T(8,128)(2,1)S(1)} %fusion.6), channel_id=1, replica_groups=mesh['integral'=8,'pair'=16] {'pair'}, dimensions={2} | all-to-all | bytes 4194304 | tf_op jit(solution)/shard_map/all_to_all | solution.py:26
  56.5 0.0 copy-start.1
  56.5 1.5 copy.23
  58.0 0.0 all-gather.2.cloned.1.call-update
  58.0 0.2 reduce-scatter.2.cloned.1.call-start
  58.3 0.2 fusion.10
  58.4 0.0 copy-done.1
  58.5 0.6 gather_fusion.1
  59.1 0.1 copy.24
  59.2 0.2 and_reduce_fusion
  59.4 0.1 reduce.2
  59.5 6.0 %fusion.14 = (bf16[4,512,1024]{2,1,0:T(8,128)(2,1)}, bf16[4,512,1024]{2,1,0:T(8,128)(2,1)}) fusion(bf16[4,1024,1024]{2,1,0:T(8,128)(2,1)} %param.5), kind=kLoop, calls=%fused_computation.41 | loop fusion | bytes 16777216 | tf_op jit(solution)/shard_map/jit(_take)/gather | solution.py:32
  65.5 5.6 %gather_fusion.2 = bf16[4,512,1024]{2,1,0:T(8,128)(2,1)} fusion(bf16[4,512,1024]{2,1,0:T(8,128)(2,1)} %get-tuple-element.9, s32[1024]{0:T(1024)S(1)} %pad_clamp_fusion), kind=kCustom, calls=%fused_computation.2 | custom fusion | bytes 8388624 | tf_op jit(solution)/shard_map/jit(_take)/gather | solution.py:32
  71.1 5.0 %gather_fusion.3 = bf16[4,512,1024]{2,1,0:T(8,128)(2,1)} fusion(bf16[4,512,1024]{2,1,0:T(8,128)(2,1)} %get-tuple-element.10, s32[1024]{0:T(1024)S(1)} %pad_clamp_fusion), kind=kCustom, calls=%fused_computation.3 | custom fusion | bytes 8388624 | tf_op jit(solution)/shard_map/jit(_take)/gather | solution.py:32
  76.2 70.5 %all-gather.2.cloned.1.call-done = bf16[2048,4,1024]{2,0,1:T(8,128)(2,1)} async-done(((bf16[2048,4,128]{2,0,1:T(8,128)(2,1)}), bf16[2048,4,1024]{2,0,1:T(8,128)(2,1)}) %all-gather.2.cloned.1.call-update) | async-done | bytes 16777232 | tf_op jit(solution)/shard_map/all_gather | solution.py:34
  146.6 24.8 %fusion.4 = f32[2048,1024]{1,0:T(8,128)} fusion(bf16[2048,4,1024]{2,0,1:T(8,128)(2,1)} %all-gather.2.cloned.1.call-done, bf16[4,512,1024]{2,1,0:T(8,128)(2,1)} %gather_fusion.3, bf16[4,512,1024]{2,1,0:T(8,128)(2,1)} %gather_fusion.2, pred[4]{0:T(512)(128)(4,1)S(1)} %get-tuple-element.7), kind=kOutput, calls=%fused_computation.9 | convolution fusion | flops 17200840704 | bytes 33554436 | tf_op jit(solution)/shard_map/dot_general | solution.py:33
  171.5 0.0 reduce-scatter.2.cloned.1.call-update
  171.5 86.2 %reduce-scatter.2.cloned.1.call-done = f32[128,1024]{1,0:T(8,128)} async-done(((f32[2048,1024]{1,0:T(8,128)}), f32[128,1024]{1,0:T(8,128)}) %reduce-scatter.2.cloned.1.call-update) | async-done | bytes 524304 | tf_op jit(solution)/shard_map/reduce_scatter | solution.py:39
  257.7 1.8 multiply_convert_fusion
  (8 shorter events, 0.1 us)
Async XLA Ops:
  6.5 1.5 copy-start
  6.5 140.1 %all-gather.2.cloned.1.call-start = ((), (), s32[]{:S(2)}) async-start(), calls=%async_computation.2 | async-start | bytes 18874368 | tf_op jit(solution)/shard_map/all_gather | solution.py:34
  56.5 1.9 copy-start.1
  58.0 199.6 %reduce-scatter.2.cloned.1.call-start = ((), (), s32[]{:S(2)}) async-start(), calls=%async_computation.3 | async-start | bytes 8912896 | tf_op jit(solution)/shard_map/reduce_scatter | solution.py:39
Sparse Core Ops, SparseCore 0:
  58.1 88.4 all-gather.1
  171.6 86.0 reduce-scatter.1
where the time goes:
time: 267 us; the launch traced here: 266 us
  waiting for transfers between devices  157 us (59%)
  blocking collectives  36.2 us (14%)
  local copies, waits for them, and re-layouts  27.8 us (10%)
  matrix products  24.8 us (9%)
  between operations  13.5 us (5%)
  other arithmetic  7.09 us (3%)
    reduce_scatter x1, waiting for transfers between devices, on_device(): lax.psum_scatter(partial_value, 'pair', scatter_dimension=0, tiled=True)  86.2 us
    all_gather x1, waiting for transfers between devices, on_device(): lax.all_gather(received, 'integral', axis=2, tiled=True)  70.5 us
    all_to_all x1, blocking collectives, on_device(): lax.all_to_all(outgoing, 'pair', split_axis=2, concat_axis=0, tiled=True)  36.2 us
    dot_general x1, matrix products, on_device(): lax.dot_general(lax.all_gather(received, 'integral', axis=2, tiled=True),...  24.8 us
    gather x3, local copies, waits for them, and re-layouts, on_device(): chosen = jnp.take(integrals, local_tile, axis=0)  16.6 us
    gather x1, local copies, waits for them, and re-layouts, on_device(): outgoing = jnp.take(t2_tiles, where_at.reshape(-1), axis=1)  8.71 us
  transfers between devices with their start and end apart: 2, of which 2 were waited for; matrix products, arithmetic and copies ran while one was open for 7% of the time, Pallas kernels for 0%

commit v1 on v0

v1 whole, which is shorter than its diff:
```python
import functools

import jax
import jax.numpy as jnp
import numpy as np
from jax import lax
from jax.experimental import pallas as pl
from jax.experimental.pallas import tpu as pltpu
from jax.sharding import Mesh
from jax.sharding import PartitionSpec as P

X, C, Y, Z = 4, 2, 4, 4
CHUNKS = (32, 32, 32, 32)
VMEM_LIMIT = 56 * 1024 * 1024


def shift(a, axis, by, n=4):
    return lax.ppermute(a, axis, [(i, (i + by) % n) for i in range(n)])


def pack_kernel(slots, keep_ref, t2_ref, *refs):
    outs, wide = refs[:-1], refs[-1]
    rows, kept, _ = t2_ref.shape
    wide[...] = t2_ref[...].astype(jnp.float32).reshape(wide.shape)
    for out in outs:
        out[...] = jnp.zeros_like(out)
    for j in range(kept):
        tile = keep_ref[j]
        owner, slot = tile // slots, tile % slots
        one = wide[pl.ds(j, rows, stride=kept), :].astype(jnp.bfloat16)
        first = 0
        for out in outs:
            count = out.shape[2]
            out[owner, slot] = one[first : first + count]
            first += count


def pack(t2, keep, owners, slots, chunks):
    rows, kept, cols = t2.shape
    return pl.pallas_call(
        functools.partial(pack_kernel, slots),
        out_shape=[jax.ShapeDtypeStruct((owners, slots, c, cols), t2.dtype) for c in chunks],
        in_specs=[pl.BlockSpec(memory_space=pltpu.SMEM), pl.BlockSpec(memory_space=pltpu.VMEM)],
        out_specs=[pl.BlockSpec(memory_space=pltpu.VMEM)] * len(chunks),
        scratch_shapes=[pltpu.VMEM((rows * kept, cols), jnp.float32)],
        compiler_params=pltpu.CompilerParams(vmem_limit_bytes=VMEM_LIMIT),
        name="pack",
    )(keep, t2)


def product_kernel(order_ref, *refs):
    pieces, b_ref, out_ref, wide = refs[:-3], refs[-3], refs[-2], refs[-1]
    groups, slots, rows, cols = pieces[0].shape
    tile = b_ref.shape[1]

    @pl.when(pl.program_id(0) == 0)
    def _():
        for i, piece in enumerate(pieces):
            for s in range(slots):
                at = pl.multiple_of(s * tile + order_ref[i] * cols, cols)
                wide[:, pl.ds(at, cols)] = piece[:, s].reshape(groups * rows, cols)

    b = b_ref[...].reshape(slots * tile, b_ref.shape[2])
    out_ref[...] = jnp.dot(wide[...], b, preferred_element_type=jnp.float32)


def product(pieces, order, integrals, step=256):
    groups, slots, rows, cols = pieces[0].shape
    _, tile, width = integrals.shape
    m, k = groups * rows, slots * tile
    whole = pl.BlockSpec(pieces[0].shape, lambda n, o: (0, 0, 0, 0))
    return pl.pallas_call(
        product_kernel,
        out_shape=jax.ShapeDtypeStruct((m, width), jnp.float32),
        grid_spec=pltpu.PrefetchScalarGridSpec(
            num_scalar_prefetch=1,
            grid=(width // step,),
            in_specs=[whole] * len(pieces) + [pl.BlockSpec((slots, tile, step), lambda n, o: (0, 0, n))],
            out_specs=pl.BlockSpec((m, step), lambda n, o: (0, n)),
            scratch_shapes=[pltpu.VMEM((m, k), integrals.dtype)],
        ),
        compiler_params=pltpu.CompilerParams(vmem_limit_bytes=VMEM_LIMIT),
        cost_estimate=pl.CostEstimate(
            flops=2 * m * k * width,
            bytes_accessed=2 * (m * k + k * width) + 4 * m * width,
            transcendentals=0,
        ),
        name="product",
    )(order, *pieces, integrals)


def on_device(t2, keep, integrals):
    slots = integrals.shape[0]
    mx, mc, my, mz = (lax.axis_index(a) for a in ("x", "c", "y", "z"))
    packed = pack(t2, keep, Y * Z, slots, CHUNKS)

    most_a = jnp.max(jnp.abs(t2)).astype(jnp.float32)
    most_b = jnp.max(jnp.abs(integrals)).astype(jnp.float32)
    most = lax.pmax(jnp.stack([most_a, most_b]), ("x", "c", "y", "z"))
    terms = slots * integrals.shape[1] * Y
    up = 15 - jnp.ceil(jnp.log2(jnp.maximum(most[0], 1e-30))) - jnp.ceil(jnp.log2(jnp.maximum(most[1], 1e-30)))
    up = jnp.clip(up - int(np.ceil(np.log2(terms))), -100, 100)
    scale, back = jnp.exp2(up), jnp.exp2(-up)

    places = [((mx + d) % X) * C + c for c in (mc, 1 - mc) for d in (0, -1, 1, 2)]
    order = jnp.stack(places).astype(jnp.int32)

    results = []
    for part in packed:
        own = lax.all_to_all(part, ("y", "z"), split_axis=0, concat_axis=0, tiled=True)
        left, right = shift(own, "x", 1), shift(own, "x", -1)
        half = own.shape[0] // 2
        far = jnp.concatenate([shift(left[:half], "x", 1), shift(right[half:], "x", -1)], axis=0)
        mine = [own, left, right, far]
        theirs = [shift(a, "c", 1, 2) for a in mine]
        partial_sum = product(mine + theirs, order, integrals)
        rows = part.shape[2]
        width = integrals.shape[2]
        scaled = (partial_sum * scale).reshape(Y, Z, rows, width)
        send = scaled.astype(jnp.float16)
        total = lax.dynamic_index_in_dim(scaled, my, 0, keepdims=False)
        for d in (1, 2, 3):
            out = lax.dynamic_index_in_dim(send, (my + d) % Y, 0, keepdims=False)
            total = total + shift(out, "y", d).astype(jnp.float32)
        result = lax.dynamic_index_in_dim(total, mz, 0, keepdims=False)
        for d in (1, 2, 3):
            out = lax.dynamic_index_in_dim(total, (mz + d) % Z, 0, keepdims=False)
            result = result + shift(out, "z", d)
        results.append(result)
    rows = jnp.concatenate(results, axis=0)
    return (rows * (0.5 * back)).astype(jnp.bfloat16)


def solution(mesh):
    fine = Mesh(mesh.devices.reshape(X, C, Y, Z), ("x", "c", "y", "z"))
    pair, integral = ("y", "z"), ("x", "c")
    placed = (P(pair, None, integral), P(), P(pair, None, integral))
    return jax.shard_map(on_device, mesh=fine, in_specs=placed, out_specs=P(pair, integral), check_vma=False)
```

time: 267 us -> 304 us (1.14)
  waiting for transfers between devices: 157 us -> 60.3 us
  blocking collectives: 36.2 us -> 98.9 us
  starting transfers between devices: 0.22 us -> 60.9 us
  Pallas kernels: 0 us -> 48.6 us
  matrix products: 24.8 us -> 0 us
  local copies, waits for them, and re-layouts: 27.8 us -> 15.2 us
  between operations: 13.5 us -> 1.98 us
  other arithmetic: 7.09 us -> 15.9 us
    reduce_scatter x1 -> x0, waiting for transfers between devices: 86.2 us -> none  [on_device(): lax.psum_scatter(partial_value, 'pair', scatter_dimension=0, tiled=True)]
    all_gather x1 -> x0, waiting for transfers between devices: 70.5 us -> none  [on_device(): lax.all_gather(received, 'integral', axis=2, tiled=True)]
    pmax x0 -> x1, blocking collectives: none -> 65.4 us  [on_device(): most = lax.pmax(jnp.stack([most_a, most_b]), ('x', 'c', 'y', 'z'))]
    ppermute x0 -> x56, starting transfers between devices: none -> 53.7 us  [shift(): return lax.ppermute(a, axis, [(i, (i + by) % n) for i in range(n)])]
    ppermute x0 -> x56, waiting for transfers between devices: none -> 52.7 us  [shift(): return lax.ppermute(a, axis, [(i, (i + by) % n) for i in range(n)])]
    pallas_call x0 -> x5, Pallas kernels: none -> 48.6 us  [the longest x4 45.2 us: product(): pl.pallas_call(product_kernel, out_shape=jax.ShapeDtypeStruct((m, width),...]
    gather x6 -> x0, local copies, waits for them, and re-layouts: 26.1 us -> none  [the longest x3 16.6 us: on_device(): chosen = jnp.take(integrals, local_tile, axis=0)]
    dot_general x1 -> x0, matrix products: 24.8 us -> none  [on_device(): lax.dot_general(lax.all_gather(received, 'integral', axis=2, tiled=True),...]
  transfers between devices with their start and end apart: 2 -> 58, of which waited for: 2 -> 21; matrix products, arithmetic and copies ran while one was open for 7% -> 9% of each run, Pallas kernels for 0% -> 15%
where the time goes in v1:
time: 304 us; the launch traced here: 302 us
  blocking collectives  98.9 us (33%)
  starting transfers between devices  60.9 us (20%)
  waiting for transfers between devices  60.3 us (20%)
  Pallas kernels  48.6 us (16%)
  other arithmetic  15.9 us (5%)
  local copies, waits for them, and re-layouts  15.2 us (5%)
    pmax x1, blocking collectives, on_device(): most = lax.pmax(jnp.stack([most_a, most_b]), ('x', 'c', 'y', 'z'))  65.4 us
    ppermute x56, starting transfers between devices, shift(): return lax.ppermute(a, axis, [(i, (i + by) % n) for i in range(n)])  53.7 us
    ppermute x56, waiting for transfers between devices, shift(): return lax.ppermute(a, axis, [(i, (i + by) % n) for i in range(n)])  52.7 us
    pallas_call x4, Pallas kernels, product(): pl.pallas_call(product_kernel, out_shape=jax.ShapeDtypeStruct((m, width),...  45.2 us
    all_to_all x2, blocking collectives, on_device(): lax.all_to_all(part, ('y', 'z'), split_axis=0, concat_axis=0, tiled=True)  33.6 us
    all_to_all x2, waiting for transfers between devices, on_device(): lax.all_to_all(part, ('y', 'z'), split_axis=0, concat_axis=0, tiled=True)  7.56 us
    all_to_all x2, starting transfers between devices, on_device(): lax.all_to_all(part, ('y', 'z'), split_axis=0, concat_axis=0, tiled=True)  7.15 us
  transfers between devices with their start and end apart: 58, of which 21 were waited for; matrix products, arithmetic and copies ran while one was open for 9% of the time, Pallas kernels for 15%

profile of v1, /device:TPU:0, one launch (start us, length us, event | category | flops | bytes accessed | tf_op | source)
XLA Modules:
  0.0 301.7 jit_solution(14419359914811568102)
XLA Ops:
  0.0 3.4 %pack.1 = (bf16[16,4,32,128]{3,2,1,0:T(8,128)(2,1)}, bf16[16,4,32,128]{3,2,1,0:T(8,128)(2,1)}, bf16[16,4,32,128]{3,2,1,0:T(8,128)(2,1)}, bf16[16,4,32,128]{3,2,1,0:T(8,128)(2,1)}) custom-call(s32[40]{0:T(128)} %keep_ref.1, bf16[128,40,128]{2,1,0:T(8,128)(2,1)} %t2_ref.1), custom_call_target="tpu_custom_call" | custom-call | tf_op jit(solution)/shard_map/pack/pallas_call | solution.py:40
  3.4 19.7 %all_to_all.20.refs_0_ = bf16[16,4,32,128]{3,2,1,0:T(8,128)(2,1)} all-to-all(bf16[16,4,32,128]{3,2,1,0:T(8,128)(2,1)} %get-tuple-element.9), channel_id=1, replica_groups=mesh['x'=4,'c'=2,'y'=4,'z'=4] {'y','z'}, dimensions={0} | all-to-all | bytes 1048576 | tf_op jit(solution)/shard_map/all_to_all | solution.py:110
  23.1 13.8 %all_to_all.21.refs_0_ = bf16[16,4,32,128]{3,2,1,0:T(8,128)(2,1)S(1)} all-to-all(bf16[16,4,32,128]{3,2,1,0:T(8,128)(2,1)} %get-tuple-element.10), channel_id=1, replica_groups=mesh['x'=4,'c'=2,'y'=4,'z'=4] {'y','z'}, dimensions={0} | all-to-all | bytes 1048576 | tf_op jit(solution)/shard_map/all_to_all | solution.py:110
  36.9 3.6 %all-to-all-start.2 = ((bf16[16,4,32,128]{3,2,1,0:T(8,128)(2,1)}), bf16[16,4,32,128]{3,2,1,0:T(8,128)(2,1)S(1)}, u32[]{:S(2)}, u32[]{:S(2)}) async-start(bf16[16,4,32,128]{3,2,1,0:T(8,128)(2,1)} %get-tuple-element.11), calls=%async_computation.2 | async-start | bytes 1048576 | tf_op jit(solution)/shard_map/all_to_all | solution.py:110
  44.1 3.0 collective-permute-start.15
  47.1 3.5 %all-to-all-done.2.refs_0_ = bf16[16,4,32,128]{3,2,1,0:T(8,128)(2,1)S(1)} async-done(((bf16[16,4,32,128]{3,2,1,0:T(8,128)(2,1)}), bf16[16,4,32,128]{3,2,1,0:T(8,128)(2,1)S(1)}, u32[]{:S(2)}, u32[]{:S(2)}) %all-to-all-start.2) | async-done | bytes 524320 | tf_op jit(solution)/shard_map/all_to_all | solution.py:110
  50.6 3.6 %all-to-all-start.3 = ((bf16[16,4,32,128]{3,2,1,0:T(8,128)(2,1)}), bf16[16,4,32,128]{3,2,1,0:T(8,128)(2,1)S(1)}, u32[]{:S(2)}, u32[]{:S(2)}) async-start(bf16[16,4,32,128]{3,2,1,0:T(8,128)(2,1)} %get-tuple-element.12), calls=%async_computation.3 | async-start | bytes 1048576 | tf_op jit(solution)/shard_map/all_to_all | solution.py:110
  54.3 2.7 collective-permute-done.refs_1_
  57.3 3.0 collective-permute-start.29
  60.2 4.0 %all-to-all-done.3.refs_0_ = bf16[16,4,32,128]{3,2,1,0:T(8,128)(2,1)S(1)} async-done(((bf16[16,4,32,128]{3,2,1,0:T(8,128)(2,1)}), bf16[16,4,32,128]{3,2,1,0:T(8,128)(2,1)S(1)}, u32[]{:S(2)}, u32[]{:S(2)}) %all-to-all-start.3) | async-done | bytes 524320 | tf_op jit(solution)/shard_map/all_to_all | solution.py:110
  64.3 4.0 %collective-permute-done.14.refs_1_ = bf16[16,4,32,128]{3,2,1,0:T(8,128)(2,1)} collective-permute-done((bf16[16,4,32,128]{3,2,1,0:T(8,128)(2,1)S(1)}, bf16[16,4,32,128]{3,2,1,0:T(8,128)(2,1)}, u32[]{:S(2)}, u32[]{:S(2)}) %collective-permute-start.14) | collective-permute-done | bytes 524320 | tf_op jit(solution)/shard_map/ppermute | solution.py:18
  68.5 3.0 collective-permute-start.43
  71.4 6.0 %abs_reduce_fusion = bf16[]{:T(256)} fusion(bf16[4,1024,1024]{2,1,0:T(8,128)(2,1)} %refs_8_.7), kind=kLoop, calls=%fused_computation | loop fusion | flops 8388607 | bytes 8388610 | tf_op jit(solution)/shard_map/reduce_max | solution.py:98
  82.5 3.0 %collective-permute-start.3 = (bf16[8,4,32,128]{3,2,1,0:T(8,128)(2,1)S(1)}, bf16[8,4,32,128]{3,2,1,0:T(8,128)(2,1)S(1)}, u32[]{:S(2)}, u32[]{:S(2)}) collective-permute-start(bf16[8,4,32,128]{3,2,1,0:T(8,128)(2,1)S(1)} %slice.41), channel_id=1, source_target_pairs={{0,96},{32,0},{64,32},{96,64},{1,97},{33,1},{65,33},{97,65},{2,98}... | collective-permute-start | bytes 786440 | tf_op jit(solution)/shard_map/ppermute | solution.py:18
  85.5 5.2 %collective-permute-done.42.refs_1_ = bf16[16,4,32,128]{3,2,1,0:T(8,128)(2,1)} collective-permute-done((bf16[16,4,32,128]{3,2,1,0:T(8,128)(2,1)S(1)}, bf16[16,4,32,128]{3,2,1,0:T(8,128)(2,1)}, u32[]{:S(2)}, u32[]{:S(2)}) %collective-permute-start.42) | collective-permute-done | bytes 524320 | tf_op jit(solution)/shard_map/ppermute | solution.py:18
  92.2 65.4 %pmax.7 = f32[2]{0:T(128)S(1)} all-reduce(f32[2]{0:T(128)S(1)} %maximum_convert_fusion), channel_id=1, replica_groups=mesh['x'=4,'c'=2,'y'=4,'z'=4] {'x','c','y','z'}, use_global_device_ids=true, to_apply=%region_2.0 | all-reduce | flops 2 | bytes 16 | tf_op jit(solution)/shard_map/pmax | solution.py:99
  164.3 2.3 collective-permute-start.17
  169.2 3.2 %collective-permute-done.17 = bf16[8,4,32,128]{3,2,1,0:T(8,128)(2,1)S(1)} collective-permute-done((bf16[8,4,32,128]{3,2,1,0:T(8,128)(2,1)S(1)}, bf16[8,4,32,128]{3,2,1,0:T(8,128)(2,1)S(1)}, u32[]{:S(2)}, u32[]{:S(2)}) %collective-permute-start.17) | collective-permute-done | bytes 262176 | tf_op jit(solution)/shard_map/ppermute | solution.py:18
  172.4 3.2 %collective-permute-start.31 = (bf16[8,4,32,128]{3,2,1,0:T(8,128)(2,1)S(1)}, bf16[8,4,32,128]{3,2,1,0:T(8,128)(2,1)S(1)}, u32[]{:S(2)}, u32[]{:S(2)}) collective-permute-start(bf16[8,4,32,128]{3,2,1,0:T(8,128)(2,1)S(1)} %slice.45), channel_id=1, source_target_pairs={{0,96},{32,0},{64,32},{96,64},{1,97},{33,1},{65,33},{97,65},{2,98}... | collective-permute-start | bytes 786440 | tf_op jit(solution)/shard_map/ppermute | solution.py:18
  175.6 2.5 collective-permute-done.30
  178.1 3.9 %collective-permute-done.44 = bf16[8,4,32,128]{3,2,1,0:T(8,128)(2,1)S(1)} collective-permute-done((bf16[8,4,32,128]{3,2,1,0:T(8,128)(2,1)S(1)}, bf16[8,4,32,128]{3,2,1,0:T(8,128)(2,1)S(1)}, u32[]{:S(2)}, u32[]{:S(2)}) %collective-permute-start.44) | collective-permute-done | bytes 262176 | tf_op jit(solution)/shard_map/ppermute | solution.py:18
  183.4 2.2 collective-permute-done.45
  188.7 11.3 %product.4 = f32[512,1024]{1,0:T(8,128)} custom-call(s32[8]{0:T(128)} %stack.49.order_ref, bf16[16,4,32,128]{3,2,1,0:T(8,128)(2,1)} %all_to_all.20.refs_0_, bf16[16,4,32,128]{3,2,1,0:T(8,128)(2,1)} %collective-permute-done.refs_1_, bf16[16,4,32,128]{3,2,1,0:T(8,128)(2,1)} %collective-permute-done.1.refs_2_, bf16[16,4,32,128]{3,2,1,0:T(8,128)(2,1)} %copy-done.9, ...), custom_call_target="tpu_custom_call" | custom-call | flops 4294967296 | bytes 14680064 | tf_op jit(solution)/shard_map/product/pallas_call | solution.py:72
  201.5 11.3 %product.5 = f32[512,1024]{1,0:T(8,128)} custom-call(s32[8]{0:T(128)} %stack.49.order_ref, bf16[16,4,32,128]{3,2,1,0:T(8,128)(2,1)} %copy-done.5, bf16[16,4,32,128]{3,2,1,0:T(8,128)(2,1)} %collective-permute-done.14.refs_1_, bf16[16,4,32,128]{3,2,1,0:T(8,128)(2,1)} %collective-permute-done.15.refs_2_, bf16[16,4,32,128]{3,2,1,0:T(8,128)(2,1)} %copy-done.8, ...), custom_call_target="tpu_custom_call" | custom-call | flops 4294967296 | bytes 14680064 | tf_op jit(solution)/shard_map/product/pallas_call | solution.py:72
  212.8 2.4 broadcast_multiply_fusion.2
  218.8 11.3 %product.6 = f32[512,1024]{1,0:T(8,128)} custom-call(s32[8]{0:T(128)} %stack.49.order_ref, bf16[16,4,32,128]{3,2,1,0:T(8,128)(2,1)} %copy-done.4, bf16[16,4,32,128]{3,2,1,0:T(8,128)(2,1)} %collective-permute-done.28.refs_1_, bf16[16,4,32,128]{3,2,1,0:T(8,128)(2,1)} %collective-permute-done.29.refs_2_, ...), custom_call_target="tpu_custom_call" | custom-call | flops 4294967296 | bytes 14680064 | tf_op jit(solution)/shard_map/product/pallas_call | solution.py:72
  236.6 11.3 %product.7 = f32[512,1024]{1,0:T(8,128)} custom-call(s32[8]{0:T(128)} %stack.49.order_ref, bf16[16,4,32,128]{3,2,1,0:T(8,128)(2,1)} %copy-done.3, bf16[16,4,32,128]{3,2,1,0:T(8,128)(2,1)} %collective-permute-done.42.refs_1_, bf16[16,4,32,128]{3,2,1,0:T(8,128)(2,1)} %collective-permute-done.43.refs_2_, bf16[16,4,32,128]{3,2,1,0:T(8,128)(2,1)} %copy-done.6, ...), custom_call_target="tpu_custom_call" | custom-call | flops 4294967296 | bytes 14680064 | tf_op jit(solution)/shard_map/product/pallas_call | solution.py:72
  258.3 6.3 %collective-permute-done.24 = f16[4,32,1024]{2,1,0:T(8,128)(2,1)S(1)} collective-permute-done((f16[4,32,1024]{2,1,0:T(8,128)(2,1)S(1)}, f16[4,32,1024]{2,1,0:T(8,128)(2,1)S(1)}, u32[]{:S(2)}, u32[]{:S(2)}) %collective-permute-start.24) | collective-permute-done | bytes 262176 | tf_op jit(solution)/shard_map/ppermute | solution.py:18
  264.8 4.1 %collective-permute-done.36 = f16[4,32,1024]{2,1,0:T(8,128)(2,1)S(1)} collective-permute-done((f16[4,32,1024]{2,1,0:T(8,128)(2,1)S(1)}, f16[4,32,1024]{2,1,0:T(8,128)(2,1)S(1)}, u32[]{:S(2)}, u32[]{:S(2)}) %collective-permute-start.36) | collective-permute-done | bytes 262176 | tf_op jit(solution)/shard_map/ppermute | solution.py:18
  269.9 5.9 %collective-permute-done.38 = f16[4,32,1024]{2,1,0:T(8,128)(2,1)S(1)} collective-permute-done((f16[4,32,1024]{2,1,0:T(8,128)(2,1)S(1)}, f16[4,32,1024]{2,1,0:T(8,128)(2,1)S(1)}, u32[]{:S(2)}, u32[]{:S(2)}) %collective-permute-start.38) | collective-permute-done | bytes 262176 | tf_op jit(solution)/shard_map/ppermute | solution.py:18
  286.9 3.5 %collective-permute-done.25 = f32[32,1024]{1,0:T(8,128)S(1)} collective-permute-done((f32[32,1024]{1,0:T(8,128)S(1)}, f32[32,1024]{1,0:T(8,128)S(1)}, u32[]{:S(2)}, u32[]{:S(2)}) %collective-permute-start.25) | collective-permute-done | bytes 131104 | tf_op jit(solution)/shard_map/ppermute | solution.py:18
  293.2 2.8 collective-permute-done.39
  (174 shorter events, 65.5 us)
Async XLA Ops:
  40.5 16.5 %collective-permute-start = (bf16[16,4,32,128]{3,2,1,0:T(8,128)(2,1)}, bf16[16,4,32,128]{3,2,1,0:T(8,128)(2,1)}, u32[]{:S(2)}, u32[]{:S(2)}) collective-permute-start(bf16[16,4,32,128]{3,2,1,0:T(8,128)(2,1)} %all_to_all.20.refs_0_), channel_id=1, source_target_pairs={{0,32},{32,64},{64,96},{96,0},{1,33},{33,65},{65,97},{97,1},{2,34}... | collective-permute-start | bytes 1572872 | tf_op jit(solution)/shard_map/ppermute | solution.py:18
  42.1 15.2 %collective-permute-start.1 = (bf16[16,4,32,128]{3,2,1,0:T(8,128)(2,1)}, bf16[16,4,32,128]{3,2,1,0:T(8,128)(2,1)}, u32[]{:S(2)}, u32[]{:S(2)}) collective-permute-start(bf16[16,4,32,128]{3,2,1,0:T(8,128)(2,1)} %all_to_all.20.refs_0_), channel_id=1, source_target_pairs={{0,96},{32,0},{64,32},{96,64},{1,97},{33,1},{65,33},{97,65},{2,98}... | collective-permute-start | bytes 1572872 | tf_op jit(solution)/shard_map/ppermute | solution.py:18
  43.8 24.4 %collective-permute-start.14 = (bf16[16,4,32,128]{3,2,1,0:T(8,128)(2,1)S(1)}, bf16[16,4,32,128]{3,2,1,0:T(8,128)(2,1)}, u32[]{:S(2)}, u32[]{:S(2)}) collective-permute-start(bf16[16,4,32,128]{3,2,1,0:T(8,128)(2,1)S(1)} %all_to_all.21.refs_0_), channel_id=1, source_target_pairs={{0,32},{32,64},{64,96},{96,0},{1,33},{33,65},{65,97},{97,1},{2,34}... | collective-permute-start | bytes 1572872 | tf_op jit(solution)/shard_map/ppermute | solution.py:18
  44.1 24.4 %collective-permute-start.15 = (bf16[16,4,32,128]{3,2,1,0:T(8,128)(2,1)S(1)}, bf16[16,4,32,128]{3,2,1,0:T(8,128)(2,1)}, u32[]{:S(2)}, u32[]{:S(2)}) collective-permute-start(bf16[16,4,32,128]{3,2,1,0:T(8,128)(2,1)S(1)} %all_to_all.21.refs_0_), channel_id=1, source_target_pairs={{0,96},{32,0},{64,32},{96,64},{1,97},{33,1},{65,33},{97,65},{2,98}... | collective-permute-start | bytes 1572872 | tf_op jit(solution)/shard_map/ppermute | solution.py:18
  54.2 113.4 %collective-permute-start.4 = (bf16[16,4,32,128]{3,2,1,0:T(8,128)(2,1)}, bf16[16,4,32,128]{3,2,1,0:T(8,128)(2,1)}, u32[]{:S(2)}, u32[]{:S(2)}) collective-permute-start(bf16[16,4,32,128]{3,2,1,0:T(8,128)(2,1)} %all_to_all.20.refs_0_), channel_id=1, source_target_pairs={{0,16},{16,0},{1,17},{17,1},{2,18},{18,2},{3,19},{19,3},{4,20},{20... | collective-permute-start | bytes 1572872 | tf_op jit(solution)/shard_map/ppermute | solution.py:18
  57.0 22.5 %collective-permute-start.28 = (bf16[16,4,32,128]{3,2,1,0:T(8,128)(2,1)S(1)}, bf16[16,4,32,128]{3,2,1,0:T(8,128)(2,1)}, u32[]{:S(2)}, u32[]{:S(2)}) collective-permute-start(bf16[16,4,32,128]{3,2,1,0:T(8,128)(2,1)S(1)} %all-to-all-done.2.refs_0_), channel_id=1, source_target_pairs={{0,32},{32,64},{64,96},{96,0},{1,33},{33,65},{65,97},{97,1},{2,34}... | collective-permute-start | bytes 1572872 | tf_op jit(solution)/shard_map/ppermute | solution.py:18
  57.3 25.2 %collective-permute-start.29 = (bf16[16,4,32,128]{3,2,1,0:T(8,128)(2,1)S(1)}, bf16[16,4,32,128]{3,2,1,0:T(8,128)(2,1)}, u32[]{:S(2)}, u32[]{:S(2)}) collective-permute-start(bf16[16,4,32,128]{3,2,1,0:T(8,128)(2,1)S(1)} %all-to-all-done.2.refs_0_), channel_id=1, source_target_pairs={{0,96},{32,0},{64,32},{96,64},{1,97},{33,1},{65,33},{97,65},{2,98}... | collective-permute-start | bytes 1572872 | tf_op jit(solution)/shard_map/ppermute | solution.py:18
  68.2 22.5 %collective-permute-start.42 = (bf16[16,4,32,128]{3,2,1,0:T(8,128)(2,1)S(1)}, bf16[16,4,32,128]{3,2,1,0:T(8,128)(2,1)}, u32[]{:S(2)}, u32[]{:S(2)}) collective-permute-start(bf16[16,4,32,128]{3,2,1,0:T(8,128)(2,1)S(1)} %all-to-all-done.3.refs_0_), channel_id=1, source_target_pairs={{0,32},{32,64},{64,96},{96,0},{1,33},{33,65},{65,97},{97,1},{2,34}... | collective-permute-start | bytes 1572872 | tf_op jit(solution)/shard_map/ppermute | solution.py:18
  68.5 95.8 %collective-permute-start.43 = (bf16[16,4,32,128]{3,2,1,0:T(8,128)(2,1)S(1)}, bf16[16,4,32,128]{3,2,1,0:T(8,128)(2,1)}, u32[]{:S(2)}, u32[]{:S(2)}) collective-permute-start(bf16[16,4,32,128]{3,2,1,0:T(8,128)(2,1)S(1)} %all-to-all-done.3.refs_0_), channel_id=1, source_target_pairs={{0,96},{32,0},{64,32},{96,64},{1,97},{33,1},{65,33},{97,65},{2,98}... | collective-permute-start | bytes 1572872 | tf_op jit(solution)/shard_map/ppermute | solution.py:18
  79.4 88.2 %collective-permute-start.2 = (bf16[8,4,32,128]{3,2,1,0:T(8,128)(2,1)}, bf16[8,4,32,128]{3,2,1,0:T(8,128)(2,1)S(1)}, u32[]{:S(2)}, u32[]{:S(2)}) collective-permute-start(bf16[8,4,32,128]{3,2,1,0:T(8,128)(2,1)} %slice.40), channel_id=1, source_target_pairs={{0,32},{32,64},{64,96},{96,0},{1,33},{33,65},{65,97},{97,1},{2,34}... | collective-permute-start | bytes 786440 | tf_op jit(solution)/shard_map/ppermute | solution.py:18
  82.5 86.0 %collective-permute-start.3 = (bf16[8,4,32,128]{3,2,1,0:T(8,128)(2,1)S(1)}, bf16[8,4,32,128]{3,2,1,0:T(8,128)(2,1)S(1)}, u32[]{:S(2)}, u32[]{:S(2)}) collective-permute-start(bf16[8,4,32,128]{3,2,1,0:T(8,128)(2,1)S(1)} %slice.41), channel_id=1, source_target_pairs={{0,96},{32,0},{64,32},{96,64},{1,97},{33,1},{65,33},{97,65},{2,98}... | collective-permute-start | bytes 786440 | tf_op jit(solution)/shard_map/ppermute | solution.py:18
  90.7 77.9 %collective-permute-start.16 = (bf16[8,4,32,128]{3,2,1,0:T(8,128)(2,1)S(1)}, bf16[8,4,32,128]{3,2,1,0:T(8,128)(2,1)S(1)}, u32[]{:S(2)}, u32[]{:S(2)}) collective-permute-start(bf16[8,4,32,128]{3,2,1,0:T(8,128)(2,1)S(1)} %slice.42), channel_id=1, source_target_pairs={{0,32},{32,64},{64,96},{96,0},{1,33},{33,65},{65,97},{97,1},{2,34}... | collective-permute-start | bytes 786440 | tf_op jit(solution)/shard_map/ppermute | solution.py:18
  168.5 17.1 %collective-permute-start.5 = (bf16[16,4,32,128]{3,2,1,0:T(8,128)(2,1)}, bf16[16,4,32,128]{3,2,1,0:T(8,128)(2,1)S(1)}, u32[]{:S(2)}, u32[]{:S(2)}) collective-permute-start(bf16[16,4,32,128]{3,2,1,0:T(8,128)(2,1)} %collective-permute-done.refs_1_), channel_id=1, source_target_pairs={{0,16},{16,0},{1,17},{17,1},{2,18},{18,2},{3,19},{19,3},{4,20},{20... | collective-permute-start | bytes 1572872 | tf_op jit(solution)/shard_map/ppermute | solution.py:18
  168.6 17.5 %collective-permute-start.6 = (bf16[16,4,32,128]{3,2,1,0:T(8,128)(2,1)}, bf16[16,4,32,128]{3,2,1,0:T(8,128)(2,1)S(1)}, u32[]{:S(2)}, u32[]{:S(2)}) collective-permute-start(bf16[16,4,32,128]{3,2,1,0:T(8,128)(2,1)} %collective-permute-done.1.refs_2_), channel_id=1, source_target_pairs={{0,16},{16,0},{1,17},{17,1},{2,18},{18,2},{3,19},{19,3},{4,20},{20... | collective-permute-start | bytes 1572872 | tf_op jit(solution)/shard_map/ppermute | solution.py:18
  182.8 17.2 %collective-permute-start.18 = (bf16[16,4,32,128]{3,2,1,0:T(8,128)(2,1)S(1)}, bf16[16,4,32,128]{3,2,1,0:T(8,128)(2,1)S(1)}, u32[]{:S(2)}, u32[]{:S(2)}) collective-permute-start(bf16[16,4,32,128]{3,2,1,0:T(8,128)(2,1)S(1)} %all_to_all.21.refs_0_), channel_id=1, source_target_pairs={{0,16},{16,0},{1,17},{17,1},{2,18},{18,2},{3,19},{19,3},{4,20},{20... | collective-permute-start | bytes 1572872 | tf_op jit(solution)/shard_map/ppermute | solution.py:18
  187.9 28.6 %collective-permute-start.32 = (bf16[16,4,32,128]{3,2,1,0:T(8,128)(2,1)S(1)}, bf16[16,4,32,128]{3,2,1,0:T(8,128)(2,1)}, u32[]{:S(2)}, u32[]{:S(2)}) collective-permute-start(bf16[16,4,32,128]{3,2,1,0:T(8,128)(2,1)S(1)} %all-to-all-done.2.refs_0_), channel_id=1, source_target_pairs={{0,16},{16,0},{1,17},{17,1},{2,18},{18,2},{3,19},{19,3},{4,20},{20... | collective-permute-start | bytes 1572872 | tf_op jit(solution)/shard_map/ppermute | solution.py:18
  200.0 30.1 %collective-permute-start.46 = (bf16[16,4,32,128]{3,2,1,0:T(8,128)(2,1)S(1)}, bf16[16,4,32,128]{3,2,1,0:T(8,128)(2,1)}, u32[]{:S(2)}, u32[]{:S(2)}) collective-permute-start(bf16[16,4,32,128]{3,2,1,0:T(8,128)(2,1)S(1)} %all-to-all-done.3.refs_0_), channel_id=1, source_target_pairs={{0,16},{16,0},{1,17},{17,1},{2,18},{18,2},{3,19},{19,3},{4,20},{20... | collective-permute-start | bytes 1572872 | tf_op jit(solution)/shard_map/ppermute | solution.py:18
  200.5 16.3 %collective-permute-start.33 = (bf16[16,4,32,128]{3,2,1,0:T(8,128)(2,1)}, bf16[16,4,32,128]{3,2,1,0:T(8,128)(2,1)}, u32[]{:S(2)}, u32[]{:S(2)}) collective-permute-start(bf16[16,4,32,128]{3,2,1,0:T(8,128)(2,1)} %collective-permute-done.28.refs_1_), channel_id=1, source_target_pairs={{0,16},{16,0},{1,17},{17,1},{2,18},{18,2},{3,19},{19,3},{4,20},{20... | collective-permute-start | bytes 1572872 | tf_op jit(solution)/shard_map/ppermute | solution.py:18
  200.6 16.3 %collective-permute-start.34 = (bf16[16,4,32,128]{3,2,1,0:T(8,128)(2,1)}, bf16[16,4,32,128]{3,2,1,0:T(8,128)(2,1)}, u32[]{:S(2)}, u32[]{:S(2)}) collective-permute-start(bf16[16,4,32,128]{3,2,1,0:T(8,128)(2,1)} %collective-permute-done.29.refs_2_), channel_id=1, source_target_pairs={{0,16},{16,0},{1,17},{17,1},{2,18},{18,2},{3,19},{19,3},{4,20},{20... | collective-permute-start | bytes 1572872 | tf_op jit(solution)/shard_map/ppermute | solution.py:18
  201.0 16.5 %collective-permute-start.35 = (bf16[16,4,32,128]{3,2,1,0:T(8,128)(2,1)}, bf16[16,4,32,128]{3,2,1,0:T(8,128)(2,1)}, u32[]{:S(2)}, u32[]{:S(2)}) collective-permute-start(bf16[16,4,32,128]{3,2,1,0:T(8,128)(2,1)} %constant_dynamic-update-slice_fusion.4.refs_3_), channel_id=1, source_target_pairs={{0,16},{16,0},{1,17},{17,1},{2,18},{18,2},{3,19},{19,3},{4,20},{20... | collective-permute-start | bytes 1572872 | tf_op jit(solution)/shard_map/ppermute | solution.py:18
  216.8 15.9 %collective-permute-start.48 = (bf16[16,4,32,128]{3,2,1,0:T(8,128)(2,1)}, bf16[16,4,32,128]{3,2,1,0:T(8,128)(2,1)S(1)}, u32[]{:S(2)}, u32[]{:S(2)}) collective-permute-start(bf16[16,4,32,128]{3,2,1,0:T(8,128)(2,1)} %collective-permute-done.43.refs_2_), channel_id=1, source_target_pairs={{0,16},{16,0},{1,17},{17,1},{2,18},{18,2},{3,19},{19,3},{4,20},{20... | collective-permute-start | bytes 1572872 | tf_op jit(solution)/shard_map/ppermute | solution.py:18
  217.0 17.3 %collective-permute-start.49 = (bf16[16,4,32,128]{3,2,1,0:T(8,128)(2,1)S(1)}, bf16[16,4,32,128]{3,2,1,0:T(8,128)(2,1)S(1)}, u32[]{:S(2)}, u32[]{:S(2)}) collective-permute-start(bf16[16,4,32,128]{3,2,1,0:T(8,128)(2,1)S(1)} %copy-done.7), channel_id=1, source_target_pairs={{0,16},{16,0},{1,17},{17,1},{2,18},{18,2},{3,19},{19,3},{4,20},{20... | collective-permute-start | bytes 1572872 | tf_op jit(solution)/shard_map/ppermute | solution.py:18
  217.5 33.0 %collective-permute-start.10 = (f16[4,32,1024]{2,1,0:T(8,128)(2,1)}, f16[4,32,1024]{2,1,0:T(8,128)(2,1)}, u32[]{:S(2)}, u32[]{:S(2)}) collective-permute-start(f16[4,32,1024]{2,1,0:T(8,128)(2,1)} %get-tuple-element.14), channel_id=1, source_target_pairs={{0,12},{4,0},{8,4},{12,8},{1,13},{5,1},{9,5},{13,9},{2,14},{6,2},{... | collective-permute-start | bytes 786440 | tf_op jit(solution)/shard_map/ppermute | solution.py:18
  230.1 22.5 %collective-permute-start.8 = (f16[4,32,1024]{2,1,0:T(8,128)(2,1)S(1)}, f16[4,32,1024]{2,1,0:T(8,128)(2,1)}, u32[]{:S(2)}, u32[]{:S(2)}) collective-permute-start(f16[4,32,1024]{2,1,0:T(8,128)(2,1)S(1)} %get-tuple-element.13), channel_id=1, source_target_pairs={{0,4},{4,8},{8,12},{12,0},{1,5},{5,9},{9,13},{13,1},{2,6},{6,10},{... | collective-permute-start | bytes 786440 | tf_op jit(solution)/shard_map/ppermute | solution.py:18
  230.9 21.9 %collective-permute-start.9 = (f16[4,32,1024]{2,1,0:T(8,128)(2,1)S(1)}, f16[4,32,1024]{2,1,0:T(8,128)(2,1)}, u32[]{:S(2)}, u32[]{:S(2)}) collective-permute-start(f16[4,32,1024]{2,1,0:T(8,128)(2,1)S(1)} %get-tuple-element.15), channel_id=1, source_target_pairs={{0,8},{4,12},{8,0},{12,4},{1,9},{5,13},{9,1},{13,5},{2,10},{6,14},... | collective-permute-start | bytes 786440 | tf_op jit(solution)/shard_map/ppermute | solution.py:18
  232.7 23.6 %collective-permute-start.22 = (f16[4,32,1024]{2,1,0:T(8,128)(2,1)S(1)}, f16[4,32,1024]{2,1,0:T(8,128)(2,1)S(1)}, u32[]{:S(2)}, u32[]{:S(2)}) collective-permute-start(f16[4,32,1024]{2,1,0:T(8,128)(2,1)S(1)} %get-tuple-element.16), channel_id=1, source_target_pairs={{0,4},{4,8},{8,12},{12,0},{1,5},{5,9},{9,13},{13,1},{2,6},{6,10},{... | collective-permute-start | bytes 786440 | tf_op jit(solution)/shard_map/ppermute | solution.py:18
  235.1 22.7 %collective-permute-start.23 = (f16[4,32,1024]{2,1,0:T(8,128)(2,1)S(1)}, f16[4,32,1024]{2,1,0:T(8,128)(2,1)S(1)}, u32[]{:S(2)}, u32[]{:S(2)}) collective-permute-start(f16[4,32,1024]{2,1,0:T(8,128)(2,1)S(1)} %get-tuple-element.18), channel_id=1, source_target_pairs={{0,8},{4,12},{8,0},{12,4},{1,9},{5,13},{9,1},{13,5},{2,10},{6,14},... | collective-permute-start | bytes 786440 | tf_op jit(solution)/shard_map/ppermute | solution.py:18
  252.7 16.1 %collective-permute-start.36 = (f16[4,32,1024]{2,1,0:T(8,128)(2,1)S(1)}, f16[4,32,1024]{2,1,0:T(8,128)(2,1)S(1)}, u32[]{:S(2)}, u32[]{:S(2)}) collective-permute-start(f16[4,32,1024]{2,1,0:T(8,128)(2,1)S(1)} %get-tuple-element.19), channel_id=1, source_target_pairs={{0,4},{4,8},{8,12},{12,0},{1,5},{5,9},{9,13},{13,1},{2,6},{6,10},{... | collective-permute-start | bytes 786440 | tf_op jit(solution)/shard_map/ppermute | solution.py:18
  252.8 16.1 %collective-permute-start.37 = (f16[4,32,1024]{2,1,0:T(8,128)(2,1)S(1)}, f16[4,32,1024]{2,1,0:T(8,128)(2,1)S(1)}, u32[]{:S(2)}, u32[]{:S(2)}) collective-permute-start(f16[4,32,1024]{2,1,0:T(8,128)(2,1)S(1)} %get-tuple-element.21), channel_id=1, source_target_pairs={{0,8},{4,12},{8,0},{12,4},{1,9},{5,13},{9,1},{13,5},{2,10},{6,14},... | collective-permute-start | bytes 786440 | tf_op jit(solution)/shard_map/ppermute | solution.py:18
  256.2 19.5 %collective-permute-start.38 = (f16[4,32,1024]{2,1,0:T(8,128)(2,1)S(1)}, f16[4,32,1024]{2,1,0:T(8,128)(2,1)S(1)}, u32[]{:S(2)}, u32[]{:S(2)}) collective-permute-start(f16[4,32,1024]{2,1,0:T(8,128)(2,1)S(1)} %get-tuple-element.20), channel_id=1, source_target_pairs={{0,12},{4,0},{8,4},{12,8},{1,13},{5,1},{9,5},{13,9},{2,14},{6,2},{... | collective-permute-start | bytes 786440 | tf_op jit(solution)/shard_map/ppermute | solution.py:18
  257.8 20.9 %collective-permute-start.50 = (f16[4,32,1024]{2,1,0:T(8,128)(2,1)S(1)}, f16[4,32,1024]{2,1,0:T(8,128)(2,1)S(1)}, u32[]{:S(2)}, u32[]{:S(2)}) collective-permute-start(f16[4,32,1024]{2,1,0:T(8,128)(2,1)S(1)} %get-tuple-element.22), channel_id=1, source_target_pairs={{0,4},{4,8},{8,12},{12,0},{1,5},{5,9},{9,13},{13,1},{2,6},{6,10},{... | collective-permute-start | bytes 786440 | tf_op jit(solution)/shard_map/ppermute | solution.py:18
  264.6 15.4 %collective-permute-start.51 = (f16[4,32,1024]{2,1,0:T(8,128)(2,1)S(1)}, f16[4,32,1024]{2,1,0:T(8,128)(2,1)S(1)}, u32[]{:S(2)}, u32[]{:S(2)}) collective-permute-start(f16[4,32,1024]{2,1,0:T(8,128)(2,1)S(1)} %get-tuple-element.24), channel_id=1, source_target_pairs={{0,8},{4,12},{8,0},{12,4},{1,9},{5,13},{9,1},{13,5},{2,10},{6,14},... | collective-permute-start | bytes 786440 | tf_op jit(solution)/shard_map/ppermute | solution.py:18
  (45 other events, 800.6 us)

commit v2 on v1

v2 whole, which is shorter than its diff:
```python
import functools

import jax
import jax.numpy as jnp
from jax import lax
from jax.experimental import pallas as pl
from jax.experimental.pallas import tpu as pltpu
from jax.sharding import Mesh
from jax.sharding import PartitionSpec as P

X, C, Y, Z = 4, 2, 4, 4
GROUPS = ((48,), (48, 32))
COLUMN_BLOCKS = 8
COST_DIV = 1
VMEM_LIMIT = 56 * 1024 * 1024
PRODUCT_VMEM = 40 * 1024 * 1024


def shift(a, axis, by, n=4):
    return lax.ppermute(a, axis, [(i, (i + by) % n) for i in range(n)])


def pack_kernel(slots, keep_ref, t2_ref, *refs):
    outs, wide = refs[:-1], refs[-1]
    rows, kept, _ = t2_ref.shape
    wide[...] = t2_ref[...].astype(jnp.float32).reshape(wide.shape)
    for out in outs:
        out[...] = jnp.zeros_like(out)
    for j in range(kept):
        tile = keep_ref[j]
        owner, slot = tile // slots, tile % slots
        one = wide[pl.ds(j, rows, stride=kept), :].astype(jnp.bfloat16)
        first = 0
        for out in outs:
            count = out.shape[2]
            out[owner, slot] = one[first : first + count]
            first += count


def pack(t2, keep, owners, slots, chunks):
    rows, kept, cols = t2.shape
    return pl.pallas_call(
        functools.partial(pack_kernel, slots),
        out_shape=[jax.ShapeDtypeStruct((owners, slots, c, cols), t2.dtype) for c in chunks],
        in_specs=[pl.BlockSpec(memory_space=pltpu.SMEM), pl.BlockSpec(memory_space=pltpu.VMEM)],
        out_specs=[pl.BlockSpec(memory_space=pltpu.VMEM)] * len(chunks),
        scratch_shapes=[pltpu.VMEM((rows * kept, cols), jnp.float32)],
        compiler_params=pltpu.CompilerParams(vmem_limit_bytes=VMEM_LIMIT),
        name="pack",
    )(keep, t2)


def product_kernel(first, halves, order_ref, *refs):
    arrays, (b_ref, out_ref, a_in, b_in, acc, sems) = list(refs[:-6]), refs[-6:]
    count, groups, slots, rows, cols = a_in.shape
    steps, deep, width = b_in.shape
    each = count // steps
    copies = []
    for i in range(count):
        t, u = i // each, i % each
        now = []
        for s in range(slots):
            span = pl.ds((u * slots + s) * cols, cols)
            at = pl.multiple_of(order_ref[i] * cols, cols)
            now.append(pltpu.make_async_copy(b_ref.at[s, pl.ds(at, cols), :], b_in.at[t, span, :], sems.at[i, s]))
        got = [arrays.pop(0)] if i not in halves else [arrays.pop(0), arrays.pop(0)]
        some = groups // len(got)
        for h, array in enumerate(got):
            begin = first if array.shape[2] > rows else 0
            source = array.at[:, :, begin : begin + rows, :]
            now.append(pltpu.make_async_copy(source, a_in.at[i, pl.ds(h * some, some)], sems.at[i, slots + h]))
        for copy in now:
            copy.start()
        copies.append(now)
    for t in range(steps):
        for now in copies[t * each : (t + 1) * each]:
            for copy in now:
                copy.wait()

        def some_columns(n, carry):
            span = pl.ds(pl.multiple_of(n * 256, 256), 256)
            a = jnp.concatenate(
                [a_in[t * each + u, :, s].reshape(groups * rows, cols) for u in range(each) for s in range(slots)], axis=1
            )
            term = jnp.dot(a, b_in[t, :, span], preferred_element_type=jnp.float32)
            if t > 0:
                term += acc[:, span]
            acc[:, span] = term
            if t == steps - 1:
                carry = jnp.maximum(carry, jnp.max(jnp.abs(term), axis=(0, 1), keepdims=True))
            return carry

        most = lax.fori_loop(0, width // 256, some_columns, jnp.zeros((1, 1), jnp.float32))
    up = 13 - jnp.floor(jnp.log2(jnp.broadcast_to(jnp.maximum(most, 2.0**-100), (8, 128))))
    scale = jnp.exp2(up)[:1]
    for n in range(width // 128):
        part = acc[:, n * 128 : (n + 1) * 128] * scale
        out_ref[:, n * rows : (n + 1) * rows, :] = part.reshape(groups, rows, 128)
    out_ref[:, width // 128 * rows :, :] = jnp.broadcast_to(up[None], (groups, 8, 128))


def product(pieces, order, integrals, first, rows, each=2):
    slots, tile, width = integrals.shape
    count, groups, cols = len(pieces), Y * Z, tile // (X * C)
    halves = tuple(i for i, piece in enumerate(pieces) if len(piece) == 2)
    arrays = [a for piece in pieces for a in piece]
    m, k = groups * rows, slots * tile
    steps = count // each
    deep = each * slots * cols
    return pl.pallas_call(
        functools.partial(product_kernel, first, halves),
        out_shape=jax.ShapeDtypeStruct((groups, width // 128 * rows + 8, 128), jnp.float32),
        in_specs=[pl.BlockSpec(memory_space=pltpu.SMEM)] + [pl.BlockSpec(memory_space=pl.ANY)] * (len(arrays) + 1),
        out_specs=pl.BlockSpec(memory_space=pltpu.VMEM),
        scratch_shapes=[
            pltpu.VMEM((count, groups, slots, rows, cols), integrals.dtype),
            pltpu.VMEM((steps, deep, width), integrals.dtype),
            pltpu.VMEM((m, width), jnp.float32),
            pltpu.SemaphoreType.DMA((count, slots + 2)),
        ],
        compiler_params=pltpu.CompilerParams(vmem_limit_bytes=PRODUCT_VMEM),
        cost_estimate=pl.CostEstimate(
            flops=2 * m * k * width // COST_DIV,
            bytes_accessed=(2 * (m * k + k * width) + 4 * m * width) // COST_DIV,
            transcendentals=0,
        ),
        name="product",
    )(order, *arrays, integrals)


def add_over_owners(sent):
    n = COLUMN_BLOCKS
    body = sent.shape[1] - 8
    rows = body // n
    got = lax.all_to_all(sent, ("y", "z"), split_axis=0, concat_axis=0, tiled=True)
    back = jnp.exp2(-got[:, body, :].astype(jnp.float32))
    total = jnp.sum(got[:, :body].astype(jnp.float32) * back[:, None, :], axis=0)
    return got, jnp.swapaxes(total.reshape(n, rows, 128), 0, 1).reshape(rows, n * 128)


def after(a, *others):
    return lax.optimization_barrier((a, *others))[0]


def swap(a):
    return shift(a, "c", 1, 2)


def on_device(t2, keep, integrals):
    slots = integrals.shape[0]
    mx, mc = lax.axis_index("x"), lax.axis_index("c")
    packed = pack(t2, keep, Y * Z, slots, [sum(g) for g in GROUPS])
    places = [((mx + d) % X) * C + c for c in (mc, 1 - mc) for d in (0, -1, 1, 2)]
    order = jnp.stack(places).astype(jnp.int32)

    results, sides, last, before = [], [], [], []
    for part, group in zip(packed, GROUPS):
        own = lax.all_to_all(part, ("y", "z"), split_axis=0, concat_axis=0, tiled=True)
        own = after(own, *sides) if sides else own
        left, right = shift(own, "x", 1), shift(own, "x", -1)
        sides = [left, right]
        near = [own, left, right]
        across = [swap(after(a, *last)) for a in near]
        first = 0
        half = own.shape[0] // 2
        for rows in group:
            span = slice(first, first + rows)
            far = [shift(left[:half, :, span], "x", 1), shift(right[half:, :, span], "x", -1)]
            far_across = [swap(after(a, *last)) for a in far]
            pieces = [[a] for a in near] + [far] + [[a] for a in across] + [far_across]
            blocks = product(pieces, order, integrals, first, rows)
            sent = blocks.astype(jnp.float16)
            last = [sent]
            got, total = add_over_owners(after(sent, *before) if before else sent)
            before = [got]
            results.append(total)
            first += rows
    return (0.5 * jnp.concatenate(results, axis=0)).astype(jnp.bfloat16)


def solution(mesh):
    fine = Mesh(mesh.devices.reshape(X, C, Y, Z), ("x", "c", "y", "z"))
    pair, integral = ("y", "z"), ("x", "c")
    placed = (P(pair, None, integral), P(), P(pair, None, integral))
    return jax.shard_map(on_device, mesh=fine, in_specs=placed, out_specs=P(pair, integral), check_vma=False)
```

time: 304 us -> 186 us (0.61)
  blocking collectives: 98.9 us -> 22.3 us
  starting transfers between devices: 60.9 us -> 35.6 us
  waiting for transfers between devices: 60.3 us -> 70 us
  Pallas kernels: 48.6 us -> 40.2 us
  local copies, waits for them, and re-layouts: 15.2 us -> 7 us
  other arithmetic: 15.9 us -> 9.94 us
    pmax x1 -> x0, blocking collectives: 65.4 us -> none  [on_device(): most = lax.pmax(jnp.stack([most_a, most_b]), ('x', 'c', 'y', 'z'))]
    ppermute x56 -> x22, starting transfers between devices: 53.7 us -> 13.8 us  [shift(): return lax.ppermute(a, axis, [(i, (i + by) % n) for i in range(n)])]
    all_to_all x0 -> x3, starting transfers between devices: none -> 18.1 us  [add_over_owners(): lax.all_to_all(sent, ('y', 'z'), split_axis=0, concat_axis=0, tiled=True)]
    all_to_all x0 -> x3, waiting for transfers between devices: none -> 14.4 us  [add_over_owners(): lax.all_to_all(sent, ('y', 'z'), split_axis=0, concat_axis=0, tiled=True)]
    all_to_all x2 -> x1, blocking collectives: 33.6 us -> 22.3 us  [on_device(): lax.all_to_all(part, ('y', 'z'), split_axis=0, concat_axis=0, tiled=True)]
    pallas_call x4 -> x3, Pallas kernels: 45.2 us -> 36.6 us  [product(): pl.pallas_call(functools.partial(product_kernel, first, halves), out_shap...]
    all_to_all x2 -> x1, waiting for transfers between devices: 7.56 us -> 0.01 us  [on_device(): lax.all_to_all(part, ('y', 'z'), split_axis=0, concat_axis=0, tiled=True)]
    reduce_max x2 -> x0, other arithmetic: 6.83 us -> none  [the longest x1 6.04 us: on_device(): most_b = jnp.max(jnp.abs(integrals)).astype(jnp.float32)]
  transfers between devices with their start and end apart: 58 -> 26, of which waited for: 21 -> 15; matrix products, arithmetic and copies ran while one was open for 9% -> 8% of each run, Pallas kernels for 15% -> 20%
where the time goes in v2:
time: 186 us; the launch traced here: 185 us
  waiting for transfers between devices  70 us (38%)
  Pallas kernels  40.2 us (22%)
  starting transfers between devices  35.6 us (19%)
  blocking collectives  22.3 us (12%)
  other arithmetic  9.94 us (5%)
  local copies, waits for them, and re-layouts  7 us (4%)
    ppermute x22, waiting for transfers between devices, shift(): return lax.ppermute(a, axis, [(i, (i + by) % n) for i in range(n)])  55.5 us
    pallas_call x3, Pallas kernels, product(): pl.pallas_call(functools.partial(product_kernel, first, halves), out_shap...  36.6 us
    all_to_all x1, blocking collectives, on_device(): lax.all_to_all(part, ('y', 'z'), split_axis=0, concat_axis=0, tiled=True)  22.3 us
    all_to_all x3, starting transfers between devices, add_over_owners(): lax.all_to_all(sent, ('y', 'z'), split_axis=0, concat_axis=0, tiled=True)  18.1 us
    all_to_all x3, waiting for transfers between devices, add_over_owners(): lax.all_to_all(sent, ('y', 'z'), split_axis=0, concat_axis=0, tiled=True)  14.4 us
    ppermute x22, starting transfers between devices, shift(): return lax.ppermute(a, axis, [(i, (i + by) % n) for i in range(n)])  13.8 us
    convert_element_type x3, other arithmetic, on_device(): sent = blocks.astype(jnp.float16)  3.92 us
  transfers between devices with their start and end apart: 26, of which 15 were waited for; matrix products, arithmetic and copies ran while one was open for 8% of the time, Pallas kernels for 20%

profile of v2, /device:TPU:0, one launch (start us, length us, event | category | flops | bytes accessed | tf_op | source)
XLA Modules:
  0.0 185.1 jit_solution(15843185525123219935)
XLA Ops:
  0.0 3.5 %pack.1 = (bf16[16,4,48,128]{3,2,1,0:T(8,128)(2,1)}, bf16[16,4,80,128]{3,2,1,0:T(8,128)(2,1)}) custom-call(s32[40]{0:T(128)} %keep_ref.1, bf16[128,40,128]{2,1,0:T(8,128)(2,1)} %t2_ref.1), custom_call_target="tpu_custom_call" | custom-call | tf_op jit(solution)/shard_map/pack/pallas_call | solution.py:42
  3.5 22.3 %all_to_all.25.refs_0_ = bf16[16,4,48,128]{3,2,1,0:T(8,128)(2,1)S(1)} all-to-all(bf16[16,4,48,128]{3,2,1,0:T(8,128)(2,1)} %get-tuple-element.17), channel_id=1, replica_groups=mesh['x'=4,'c'=2,'y'=4,'z'=4] {'y','z'}, dimensions={0} | all-to-all | bytes 1572864 | tf_op jit(solution)/shard_map/all_to_all | solution.py:158
  25.8 1.5 collective-permute-start
  27.3 3.7 %all-to-all-start.2 = ((bf16[16,4,80,128]{3,2,1,0:T(8,128)(2,1)}), bf16[16,4,80,128]{3,2,1,0:T(8,128)(2,1)S(1)}, u32[]{:S(2)}, u32[]{:S(2)}) async-start(bf16[16,4,80,128]{3,2,1,0:T(8,128)(2,1)} %get-tuple-element.18), calls=%async_computation.2 | async-start | bytes 2621440 | tf_op jit(solution)/shard_map/all_to_all | solution.py:158
  31.0 1.8 collective-permute-start.1
  32.8 12.5 %collective-permute-done.refs_1_ = bf16[16,4,48,128]{3,2,1,0:T(8,128)(2,1)} collective-permute-done((bf16[16,4,48,128]{3,2,1,0:T(8,128)(2,1)S(1)}, bf16[16,4,48,128]{3,2,1,0:T(8,128)(2,1)}, u32[]{:S(2)}, u32[]{:S(2)}) %collective-permute-start) | collective-permute-done | bytes 786464 | tf_op jit(solution)/shard_map/ppermute | solution.py:20
  46.7 2.4 %collective-permute-done.1.refs_2_ = bf16[16,4,48,128]{3,2,1,0:T(8,128)(2,1)} collective-permute-done((bf16[16,4,48,128]{3,2,1,0:T(8,128)(2,1)S(1)}, bf16[16,4,48,128]{3,2,1,0:T(8,128)(2,1)}, u32[]{:S(2)}, u32[]{:S(2)}) %collective-permute-start.1) | collective-permute-done | bytes 786464 | tf_op jit(solution)/shard_map/ppermute | solution.py:20
  49.1 1.8 slice.49
  50.9 3.0 %collective-permute-start.3 = (bf16[8,4,48,128]{3,2,1,0:T(8,128)(2,1)}, bf16[8,4,48,128]{3,2,1,0:T(8,128)(2,1)}, u32[]{:S(2)}, u32[]{:S(2)}) collective-permute-start(bf16[8,4,48,128]{3,2,1,0:T(8,128)(2,1)} %slice.49), channel_id=1, source_target_pairs={{0,96},{32,0},{64,32},{96,64},{1,97},{33,1},{65,33},{97,65},{2,98}... | collective-permute-start | bytes 1179656 | tf_op jit(solution)/shard_map/ppermute | solution.py:20
  53.9 2.8 %collective-permute-done.2.refs_3_ = bf16[8,4,48,128]{3,2,1,0:T(8,128)(2,1)} collective-permute-done((bf16[8,4,48,128]{3,2,1,0:T(8,128)(2,1)S(1)}, bf16[8,4,48,128]{3,2,1,0:T(8,128)(2,1)}, u32[]{:S(2)}, u32[]{:S(2)}) %collective-permute-start.2) | collective-permute-done | bytes 393248 | tf_op jit(solution)/shard_map/ppermute | solution.py:20
  58.4 3.1 %collective-permute-done.3.refs_4_ = bf16[8,4,48,128]{3,2,1,0:T(8,128)(2,1)} collective-permute-done((bf16[8,4,48,128]{3,2,1,0:T(8,128)(2,1)}, bf16[8,4,48,128]{3,2,1,0:T(8,128)(2,1)}, u32[]{:S(2)}, u32[]{:S(2)}) %collective-permute-start.3) | collective-permute-done | bytes 393248 | tf_op jit(solution)/shard_map/ppermute | solution.py:20
  62.3 2.0 %collective-permute-done.8.refs_9_ = bf16[8,4,48,128]{3,2,1,0:T(8,128)(2,1)} collective-permute-done((bf16[8,4,48,128]{3,2,1,0:T(8,128)(2,1)}, bf16[8,4,48,128]{3,2,1,0:T(8,128)(2,1)}, u32[]{:S(2)}, u32[]{:S(2)}) %collective-permute-start.8) | collective-permute-done | bytes 393248 | tf_op jit(solution)/shard_map/ppermute | solution.py:20
  65.5 13.0 %product.3 = f32[16,392,128]{2,1,0:T(8,128)S(1)} custom-call(s32[8]{0:T(128)S(1)} %stack.35.order_ref, bf16[16,4,48,128]{3,2,1,0:T(8,128)(2,1)S(1)} %all_to_all.25.refs_0_, bf16[16,4,48,128]{3,2,1,0:T(8,128)(2,1)} %collective-permute-done.refs_1_, bf16[16,4,48,128]{3,2,1,0:T(8,128)(2,1)} %collective-permute-done.1.refs_2_, ...), custom_call_target="tpu_custom_call" | custom-call | flops 6442450944 | bytes 17825792 | tf_op jit(solution)/shard_map/product/pallas_call | solution.py:110
  80.0 9.2 %collective-permute-done.10.refs_2_ = bf16[16,4,80,128]{3,2,1,0:T(8,128)(2,1)S(1)} collective-permute-done((bf16[16,4,80,128]{3,2,1,0:T(8,128)(2,1)S(1)}, bf16[16,4,80,128]{3,2,1,0:T(8,128)(2,1)S(1)}, u32[]{:S(2)}, u32[]{:S(2)}) %collective-permute-start.10) | collective-permute-done | bytes 1310752 | tf_op jit(solution)/shard_map/ppermute | solution.py:20
  89.2 1.4 collective-permute-done.9.refs_1_
  90.6 5.3 %all-to-all-start.1 = ((f16[16,392,128]{2,1,0:T(8,128)(2,1)}), f16[16,392,128]{2,1,0:T(8,128)(2,1)}, u32[]{:S(2)}, u32[]{:S(2)}) async-start(f16[16,392,128]{2,1,0:T(8,128)(2,1)} %convert_element_type.33), calls=%async_computation.1 | async-start | bytes 3211264 | tf_op jit(solution)/shard_map/all_to_all | solution.py:135
  96.0 3.2 %collective-permute-start.12 = (bf16[8,4,48,128]{3,2,1,0:T(8,128)(2,1)S(1)}, bf16[8,4,48,128]{3,2,1,0:T(8,128)(2,1)S(1)}, u32[]{:S(2)}, u32[]{:S(2)}) collective-permute-start(bf16[8,4,48,128]{3,2,1,0:T(8,128)(2,1)S(1)} %slice.53), channel_id=1, source_target_pairs={{0,96},{32,0},{64,32},{96,64},{1,97},{33,1},{65,33},{97,65},{2,98}... | collective-permute-start | bytes 1179656 | tf_op jit(solution)/shard_map/ppermute | solution.py:20
  100.3 7.2 %collective-permute-done.12.refs_4_ = bf16[8,4,48,128]{3,2,1,0:T(8,128)(2,1)S(1)} collective-permute-done((bf16[8,4,48,128]{3,2,1,0:T(8,128)(2,1)S(1)}, bf16[8,4,48,128]{3,2,1,0:T(8,128)(2,1)S(1)}, u32[]{:S(2)}, u32[]{:S(2)}) %collective-permute-start.12) | collective-permute-done | bytes 393248 | tf_op jit(solution)/shard_map/ppermute | solution.py:20
  107.4 4.5 %collective-permute-done.11.refs_3_ = bf16[8,4,48,128]{3,2,1,0:T(8,128)(2,1)S(1)} collective-permute-done((bf16[8,4,48,128]{3,2,1,0:T(8,128)(2,1)S(1)}, bf16[8,4,48,128]{3,2,1,0:T(8,128)(2,1)S(1)}, u32[]{:S(2)}, u32[]{:S(2)}) %collective-permute-start.11) | collective-permute-done | bytes 393248 | tf_op jit(solution)/shard_map/ppermute | solution.py:20
  111.9 1.7 collective-permute-done.16.refs_8_
  113.6 13.0 %product.4 = f32[16,392,128]{2,1,0:T(8,128)S(1)} custom-call(s32[8]{0:T(128)S(1)} %stack.35.order_ref, bf16[16,4,80,128]{3,2,1,0:T(8,128)(2,1)S(1)} %all-to-all-done.2.refs_0_, bf16[16,4,80,128]{3,2,1,0:T(8,128)(2,1)} %collective-permute-done.9.refs_1_, bf16[16,4,80,128]{3,2,1,0:T(8,128)(2,1)S(1)} %collective-permute-done.10.refs_2_, ...), custom_call_target="tpu_custom_call" | custom-call | flops 6442450944 | bytes 17825792 | tf_op jit(solution)/shard_map/product/pallas_call | solution.py:110
  126.7 1.4 convert_element_type.36
  128.1 6.9 %all-to-all-start.3 = ((f16[16,392,128]{2,1,0:T(8,128)(2,1)}), f16[16,392,128]{2,1,0:T(8,128)(2,1)}, u32[]{:S(2)}, u32[]{:S(2)}) async-start(f16[16,392,128]{2,1,0:T(8,128)(2,1)} %convert_element_type.36), calls=%async_computation.3 | async-start | bytes 3211264 | tf_op jit(solution)/shard_map/all_to_all | solution.py:135
  136.1 2.1 %collective-permute-start.18 = (bf16[8,4,32,128]{3,2,1,0:T(8,128)(2,1)S(1)}, bf16[8,4,32,128]{3,2,1,0:T(8,128)(2,1)S(1)}, u32[]{:S(2)}, u32[]{:S(2)}) collective-permute-start(bf16[8,4,32,128]{3,2,1,0:T(8,128)(2,1)S(1)} %slice.56), channel_id=1, source_target_pairs={{0,32},{32,64},{64,96},{96,0},{1,33},{33,65},{65,97},{97,1},{2,34}... | collective-permute-start | bytes 786440 | tf_op jit(solution)/shard_map/ppermute | solution.py:20
  138.2 5.0 %collective-permute-done.19.refs_4_ = bf16[8,4,32,128]{3,2,1,0:T(8,128)(2,1)S(1)} collective-permute-done((bf16[8,4,32,128]{3,2,1,0:T(8,128)(2,1)S(1)}, bf16[8,4,32,128]{3,2,1,0:T(8,128)(2,1)S(1)}, u32[]{:S(2)}, u32[]{:S(2)}) %collective-permute-start.19) | collective-permute-done | bytes 262176 | tf_op jit(solution)/shard_map/ppermute | solution.py:20
  143.1 2.3 %collective-permute-done.18.refs_3_ = bf16[8,4,32,128]{3,2,1,0:T(8,128)(2,1)S(1)} collective-permute-done((bf16[8,4,32,128]{3,2,1,0:T(8,128)(2,1)S(1)}, bf16[8,4,32,128]{3,2,1,0:T(8,128)(2,1)S(1)}, u32[]{:S(2)}, u32[]{:S(2)}) %collective-permute-start.18) | collective-permute-done | bytes 262176 | tf_op jit(solution)/shard_map/ppermute | solution.py:20
  145.4 1.5 collective-permute-done.20.refs_8_
  147.0 10.6 %product.5 = f32[16,264,128]{2,1,0:T(8,128)S(1)} custom-call(s32[8]{0:T(128)S(1)} %stack.35.order_ref, bf16[16,4,80,128]{3,2,1,0:T(8,128)(2,1)S(1)} %all-to-all-done.2.refs_0_, bf16[16,4,80,128]{3,2,1,0:T(8,128)(2,1)} %collective-permute-done.9.refs_1_, bf16[16,4,80,128]{3,2,1,0:T(8,128)(2,1)S(1)} %collective-permute-done.10.refs_2_, ...), custom_call_target="tpu_custom_call" | custom-call | flops 4294967296 | bytes 14680064 | tf_op jit(solution)/shard_map/product/pallas_call | solution.py:110
  159.8 5.9 %all-to-all-start.4 = ((f16[16,264,128]{2,1,0:T(8,128)(2,1)}), f16[16,264,128]{2,1,0:T(8,128)(2,1)S(1)}, u32[]{:S(2)}, u32[]{:S(2)}) async-start(f16[16,264,128]{2,1,0:T(8,128)(2,1)} %convert_element_type.39), calls=%async_computation.4 | async-start | bytes 2162688 | tf_op jit(solution)/shard_map/all_to_all | solution.py:135
  166.4 1.7 multiply_reduce_fusion.1
  169.0 1.7 multiply_reduce_fusion
  170.8 13.4 %all-to-all-done.4 = f16[16,264,128]{2,1,0:T(8,128)(2,1)S(1)} async-done(((f16[16,264,128]{2,1,0:T(8,128)(2,1)}), f16[16,264,128]{2,1,0:T(8,128)(2,1)S(1)}, u32[]{:S(2)}, u32[]{:S(2)}) %all-to-all-start.4) | async-done | bytes 1081376 | tf_op jit(solution)/shard_map/all_to_all | solution.py:135
  (49 shorter events, 13.6 us)
Async XLA Ops:
  25.8 19.6 %collective-permute-start = (bf16[16,4,48,128]{3,2,1,0:T(8,128)(2,1)S(1)}, bf16[16,4,48,128]{3,2,1,0:T(8,128)(2,1)}, u32[]{:S(2)}, u32[]{:S(2)}) collective-permute-start(bf16[16,4,48,128]{3,2,1,0:T(8,128)(2,1)S(1)} %all_to_all.25.refs_0_), channel_id=1, source_target_pairs={{0,32},{32,64},{64,96},{96,0},{1,33},{33,65},{65,97},{97,1},{2,34}... | collective-permute-start | bytes 2359304 | tf_op jit(solution)/shard_map/ppermute | solution.py:20
  27.3 29.9 %all-to-all-start.2 = ((bf16[16,4,80,128]{3,2,1,0:T(8,128)(2,1)}), bf16[16,4,80,128]{3,2,1,0:T(8,128)(2,1)S(1)}, u32[]{:S(2)}, u32[]{:S(2)}) async-start(bf16[16,4,80,128]{3,2,1,0:T(8,128)(2,1)} %get-tuple-element.18), calls=%async_computation.2 | async-start | bytes 2621440 | tf_op jit(solution)/shard_map/all_to_all | solution.py:158
  31.0 18.1 %collective-permute-start.1 = (bf16[16,4,48,128]{3,2,1,0:T(8,128)(2,1)S(1)}, bf16[16,4,48,128]{3,2,1,0:T(8,128)(2,1)}, u32[]{:S(2)}, u32[]{:S(2)}) collective-permute-start(bf16[16,4,48,128]{3,2,1,0:T(8,128)(2,1)S(1)} %all_to_all.25.refs_0_), channel_id=1, source_target_pairs={{0,96},{32,0},{64,32},{96,64},{1,97},{33,1},{65,33},{97,65},{2,98}... | collective-permute-start | bytes 2359304 | tf_op jit(solution)/shard_map/ppermute | solution.py:20
  32.8 24.4 %collective-permute-start.4 = (bf16[16,4,48,128]{3,2,1,0:T(8,128)(2,1)S(1)}, bf16[16,4,48,128]{3,2,1,0:T(8,128)(2,1)S(1)}, u32[]{:S(2)}, u32[]{:S(2)}) collective-permute-start(bf16[16,4,48,128]{3,2,1,0:T(8,128)(2,1)S(1)} %all_to_all.25.refs_0_), channel_id=1, source_target_pairs={{0,16},{16,0},{1,17},{17,1},{2,18},{18,2},{3,19},{19,3},{4,20},{20... | collective-permute-start | bytes 2359304 | tf_op jit(solution)/shard_map/ppermute | solution.py:20
  46.3 10.3 %collective-permute-start.2 = (bf16[8,4,48,128]{3,2,1,0:T(8,128)(2,1)S(1)}, bf16[8,4,48,128]{3,2,1,0:T(8,128)(2,1)}, u32[]{:S(2)}, u32[]{:S(2)}) collective-permute-start(bf16[8,4,48,128]{3,2,1,0:T(8,128)(2,1)S(1)} %slice.48), channel_id=1, source_target_pairs={{0,32},{32,64},{64,96},{96,0},{1,33},{33,65},{65,97},{97,1},{2,34}... | collective-permute-start | bytes 1179656 | tf_op jit(solution)/shard_map/ppermute | solution.py:20
  50.9 10.5 %collective-permute-start.3 = (bf16[8,4,48,128]{3,2,1,0:T(8,128)(2,1)}, bf16[8,4,48,128]{3,2,1,0:T(8,128)(2,1)}, u32[]{:S(2)}, u32[]{:S(2)}) collective-permute-start(bf16[8,4,48,128]{3,2,1,0:T(8,128)(2,1)} %slice.49), channel_id=1, source_target_pairs={{0,96},{32,0},{64,32},{96,64},{1,97},{33,1},{65,33},{97,65},{2,98}... | collective-permute-start | bytes 1179656 | tf_op jit(solution)/shard_map/ppermute | solution.py:20
  56.6 5.6 %collective-permute-start.7 = (bf16[8,4,48,128]{3,2,1,0:T(8,128)(2,1)}, bf16[8,4,48,128]{3,2,1,0:T(8,128)(2,1)}, u32[]{:S(2)}, u32[]{:S(2)}) collective-permute-start(bf16[8,4,48,128]{3,2,1,0:T(8,128)(2,1)} %collective-permute-done.2.refs_3_), channel_id=1, source_target_pairs={{0,16},{16,0},{1,17},{17,1},{2,18},{18,2},{3,19},{19,3},{4,20},{20... | collective-permute-start | bytes 1179656 | tf_op jit(solution)/shard_map/ppermute | solution.py:20
  56.6 7.7 %collective-permute-start.5 = (bf16[16,4,48,128]{3,2,1,0:T(8,128)(2,1)}, bf16[16,4,48,128]{3,2,1,0:T(8,128)(2,1)}, u32[]{:S(2)}, u32[]{:S(2)}) collective-permute-start(bf16[16,4,48,128]{3,2,1,0:T(8,128)(2,1)} %collective-permute-done.refs_1_), channel_id=1, source_target_pairs={{0,16},{16,0},{1,17},{17,1},{2,18},{18,2},{3,19},{19,3},{4,20},{20... | collective-permute-start | bytes 2359304 | tf_op jit(solution)/shard_map/ppermute | solution.py:20
  57.1 7.2 %collective-permute-start.6 = (bf16[16,4,48,128]{3,2,1,0:T(8,128)(2,1)}, bf16[16,4,48,128]{3,2,1,0:T(8,128)(2,1)}, u32[]{:S(2)}, u32[]{:S(2)}) collective-permute-start(bf16[16,4,48,128]{3,2,1,0:T(8,128)(2,1)} %collective-permute-done.1.refs_2_), channel_id=1, source_target_pairs={{0,16},{16,0},{1,17},{17,1},{2,18},{18,2},{3,19},{19,3},{4,20},{20... | collective-permute-start | bytes 2359304 | tf_op jit(solution)/shard_map/ppermute | solution.py:20
  57.1 0.9 copy-start
  58.0 31.2 %collective-permute-start.10 = (bf16[16,4,80,128]{3,2,1,0:T(8,128)(2,1)S(1)}, bf16[16,4,80,128]{3,2,1,0:T(8,128)(2,1)S(1)}, u32[]{:S(2)}, u32[]{:S(2)}) collective-permute-start(bf16[16,4,80,128]{3,2,1,0:T(8,128)(2,1)S(1)} %all-to-all-done.2.refs_0_), channel_id=1, source_target_pairs={{0,96},{32,0},{64,32},{96,64},{1,97},{33,1},{65,33},{97,65},{2,98}... | collective-permute-start | bytes 3932168 | tf_op jit(solution)/shard_map/ppermute | solution.py:20
  61.4 29.2 %collective-permute-start.9 = (bf16[16,4,80,128]{3,2,1,0:T(8,128)(2,1)S(1)}, bf16[16,4,80,128]{3,2,1,0:T(8,128)(2,1)}, u32[]{:S(2)}, u32[]{:S(2)}) collective-permute-start(bf16[16,4,80,128]{3,2,1,0:T(8,128)(2,1)S(1)} %all-to-all-done.2.refs_0_), channel_id=1, source_target_pairs={{0,32},{32,64},{64,96},{96,0},{1,33},{33,65},{65,97},{97,1},{2,34}... | collective-permute-start | bytes 3932168 | tf_op jit(solution)/shard_map/ppermute | solution.py:20
  62.3 2.1 %collective-permute-start.8 = (bf16[8,4,48,128]{3,2,1,0:T(8,128)(2,1)}, bf16[8,4,48,128]{3,2,1,0:T(8,128)(2,1)}, u32[]{:S(2)}, u32[]{:S(2)}) collective-permute-start(bf16[8,4,48,128]{3,2,1,0:T(8,128)(2,1)} %collective-permute-done.3.refs_4_), channel_id=1, source_target_pairs={{0,16},{16,0},{1,17},{17,1},{2,18},{18,2},{3,19},{19,3},{4,20},{20... | collective-permute-start | bytes 1179656 | tf_op jit(solution)/shard_map/ppermute | solution.py:20
  64.3 1.1 copy-start.1
  79.8 32.1 %collective-permute-start.13 = (bf16[16,4,80,128]{3,2,1,0:T(8,128)(2,1)S(1)}, bf16[16,4,80,128]{3,2,1,0:T(8,128)(2,1)}, u32[]{:S(2)}, u32[]{:S(2)}) collective-permute-start(bf16[16,4,80,128]{3,2,1,0:T(8,128)(2,1)S(1)} %all-to-all-done.2.refs_0_), channel_id=1, source_target_pairs={{0,16},{16,0},{1,17},{17,1},{2,18},{18,2},{3,19},{19,3},{4,20},{20... | collective-permute-start | bytes 3932168 | tf_op jit(solution)/shard_map/ppermute | solution.py:20
  89.2 24.4 %collective-permute-start.15 = (bf16[16,4,80,128]{3,2,1,0:T(8,128)(2,1)S(1)}, bf16[16,4,80,128]{3,2,1,0:T(8,128)(2,1)}, u32[]{:S(2)}, u32[]{:S(2)}) collective-permute-start(bf16[16,4,80,128]{3,2,1,0:T(8,128)(2,1)S(1)} %collective-permute-done.10.refs_2_), channel_id=1, source_target_pairs={{0,16},{16,0},{1,17},{17,1},{2,18},{18,2},{3,19},{19,3},{4,20},{20... | collective-permute-start | bytes 3932168 | tf_op jit(solution)/shard_map/ppermute | solution.py:20
  90.6 23.1 %collective-permute-start.14 = (bf16[16,4,80,128]{3,2,1,0:T(8,128)(2,1)}, bf16[16,4,80,128]{3,2,1,0:T(8,128)(2,1)}, u32[]{:S(2)}, u32[]{:S(2)}) collective-permute-start(bf16[16,4,80,128]{3,2,1,0:T(8,128)(2,1)} %collective-permute-done.9.refs_1_), channel_id=1, source_target_pairs={{0,16},{16,0},{1,17},{17,1},{2,18},{18,2},{3,19},{19,3},{4,20},{20... | collective-permute-start | bytes 3932168 | tf_op jit(solution)/shard_map/ppermute | solution.py:20
  90.6 37.5 %all-to-all-start.1 = ((f16[16,392,128]{2,1,0:T(8,128)(2,1)}), f16[16,392,128]{2,1,0:T(8,128)(2,1)}, u32[]{:S(2)}, u32[]{:S(2)}) async-start(f16[16,392,128]{2,1,0:T(8,128)(2,1)} %convert_element_type.33), calls=%async_computation.1 | async-start | bytes 3211264 | tf_op jit(solution)/shard_map/all_to_all | solution.py:135
  96.0 11.4 %collective-permute-start.12 = (bf16[8,4,48,128]{3,2,1,0:T(8,128)(2,1)S(1)}, bf16[8,4,48,128]{3,2,1,0:T(8,128)(2,1)S(1)}, u32[]{:S(2)}, u32[]{:S(2)}) collective-permute-start(bf16[8,4,48,128]{3,2,1,0:T(8,128)(2,1)S(1)} %slice.53), channel_id=1, source_target_pairs={{0,96},{32,0},{64,32},{96,64},{1,97},{33,1},{65,33},{97,65},{2,98}... | collective-permute-start | bytes 1179656 | tf_op jit(solution)/shard_map/ppermute | solution.py:20
  100.2 11.7 %collective-permute-start.11 = (bf16[8,4,48,128]{3,2,1,0:T(8,128)(2,1)S(1)}, bf16[8,4,48,128]{3,2,1,0:T(8,128)(2,1)S(1)}, u32[]{:S(2)}, u32[]{:S(2)}) collective-permute-start(bf16[8,4,48,128]{3,2,1,0:T(8,128)(2,1)S(1)} %slice.52), channel_id=1, source_target_pairs={{0,32},{32,64},{64,96},{96,0},{1,33},{33,65},{65,97},{97,1},{2,34}... | collective-permute-start | bytes 1179656 | tf_op jit(solution)/shard_map/ppermute | solution.py:20
  107.4 4.5 %collective-permute-start.17 = (bf16[8,4,48,128]{3,2,1,0:T(8,128)(2,1)S(1)}, bf16[8,4,48,128]{3,2,1,0:T(8,128)(2,1)S(1)}, u32[]{:S(2)}, u32[]{:S(2)}) collective-permute-start(bf16[8,4,48,128]{3,2,1,0:T(8,128)(2,1)S(1)} %collective-permute-done.12.refs_4_), channel_id=1, source_target_pairs={{0,16},{16,0},{1,17},{17,1},{2,18},{18,2},{3,19},{19,3},{4,20},{20... | collective-permute-start | bytes 1179656 | tf_op jit(solution)/shard_map/ppermute | solution.py:20
  111.9 1.7 collective-permute-start.16
  128.1 31.7 %all-to-all-start.3 = ((f16[16,392,128]{2,1,0:T(8,128)(2,1)}), f16[16,392,128]{2,1,0:T(8,128)(2,1)}, u32[]{:S(2)}, u32[]{:S(2)}) async-start(f16[16,392,128]{2,1,0:T(8,128)(2,1)} %convert_element_type.36), calls=%async_computation.3 | async-start | bytes 3211264 | tf_op jit(solution)/shard_map/all_to_all | solution.py:135
  135.0 8.1 %collective-permute-start.19 = (bf16[8,4,32,128]{3,2,1,0:T(8,128)(2,1)S(1)}, bf16[8,4,32,128]{3,2,1,0:T(8,128)(2,1)S(1)}, u32[]{:S(2)}, u32[]{:S(2)}) collective-permute-start(bf16[8,4,32,128]{3,2,1,0:T(8,128)(2,1)S(1)} %slice.57), channel_id=1, source_target_pairs={{0,96},{32,0},{64,32},{96,64},{1,97},{33,1},{65,33},{97,65},{2,98}... | collective-permute-start | bytes 786440 | tf_op jit(solution)/shard_map/ppermute | solution.py:20
  136.1 9.3 %collective-permute-start.18 = (bf16[8,4,32,128]{3,2,1,0:T(8,128)(2,1)S(1)}, bf16[8,4,32,128]{3,2,1,0:T(8,128)(2,1)S(1)}, u32[]{:S(2)}, u32[]{:S(2)}) collective-permute-start(bf16[8,4,32,128]{3,2,1,0:T(8,128)(2,1)S(1)} %slice.56), channel_id=1, source_target_pairs={{0,32},{32,64},{64,96},{96,0},{1,33},{33,65},{65,97},{97,1},{2,34}... | collective-permute-start | bytes 786440 | tf_op jit(solution)/shard_map/ppermute | solution.py:20
  143.1 2.3 %collective-permute-start.21 = (bf16[8,4,32,128]{3,2,1,0:T(8,128)(2,1)S(1)}, bf16[8,4,32,128]{3,2,1,0:T(8,128)(2,1)S(1)}, u32[]{:S(2)}, u32[]{:S(2)}) collective-permute-start(bf16[8,4,32,128]{3,2,1,0:T(8,128)(2,1)S(1)} %collective-permute-done.19.refs_4_), channel_id=1, source_target_pairs={{0,16},{16,0},{1,17},{17,1},{2,18},{18,2},{3,19},{19,3},{4,20},{20... | collective-permute-start | bytes 786440 | tf_op jit(solution)/shard_map/ppermute | solution.py:20
  145.4 1.5 collective-permute-start.20
  159.8 24.4 %all-to-all-start.4 = ((f16[16,264,128]{2,1,0:T(8,128)(2,1)}), f16[16,264,128]{2,1,0:T(8,128)(2,1)S(1)}, u32[]{:S(2)}, u32[]{:S(2)}) async-start(f16[16,264,128]{2,1,0:T(8,128)(2,1)} %convert_element_type.39), calls=%async_computation.4 | async-start | bytes 2162688 | tf_op jit(solution)/shard_map/all_to_all | solution.py:135

commit v3 on v2

--- a/solution.py
+++ b/solution.py
@@ -9,9 +9,11 @@
 from jax.sharding import PartitionSpec as P
 
 X, C, Y, Z = 4, 2, 4, 4
-GROUPS = ((48,), (48, 32))
+GROUPS = (64, 64)
+BY_FAR = True
+NEAR_FREE = True
 COLUMN_BLOCKS = 8
-COST_DIV = 1
+STEP = 512
 VMEM_LIMIT = 56 * 1024 * 1024
 PRODUCT_VMEM = 40 * 1024 * 1024
 
@@ -50,7 +52,7 @@
     )(keep, t2)
 
 
-def product_kernel(first, halves, order_ref, *refs):
+def product_kernel(halves, order_ref, *refs):
     arrays, (b_ref, out_ref, a_in, b_in, acc, sems) = list(refs[:-6]), refs[-6:]
     count, groups, slots, rows, cols = a_in.shape
     steps, deep, width = b_in.shape
@@ -66,9 +68,7 @@
         got = [arrays.pop(0)] if i not in halves else [arrays.pop(0), arrays.pop(0)]
         some = groups // len(got)
         for h, array in enumerate(got):
-            begin = first if array.shape[2] > rows else 0
-            source = array.at[:, :, begin : begin + rows, :]
-            now.append(pltpu.make_async_copy(source, a_in.at[i, pl.ds(h * some, some)], sems.at[i, slots + h]))
+            now.append(pltpu.make_async_copy(array, a_in.at[i, pl.ds(h * some, some)], sems.at[i, slots + h]))
         for copy in now:
             copy.start()
         copies.append(now)
@@ -78,7 +78,7 @@
                 copy.wait()
 
         def some_columns(n, carry):
-            span = pl.ds(pl.multiple_of(n * 256, 256), 256)
+            span = pl.ds(pl.multiple_of(n * STEP, STEP), STEP)
             a = jnp.concatenate(
                 [a_in[t * each + u, :, s].reshape(groups * rows, cols) for u in range(each) for s in range(slots)], axis=1
             )
@@ -90,7 +90,7 @@
                 carry = jnp.maximum(carry, jnp.max(jnp.abs(term), axis=(0, 1), keepdims=True))
             return carry
 
-        most = lax.fori_loop(0, width // 256, some_columns, jnp.zeros((1, 1), jnp.float32))
+        most = lax.fori_loop(0, width // STEP, some_columns, jnp.zeros((1, 1), jnp.float32))
     up = 13 - jnp.floor(jnp.log2(jnp.broadcast_to(jnp.maximum(most, 2.0**-100), (8, 128))))
     scale = jnp.exp2(up)[:1]
     for n in range(width // 128):
@@ -99,16 +99,17 @@
     out_ref[:, width // 128 * rows :, :] = jnp.broadcast_to(up[None], (groups, 8, 128))
 
 
-def product(pieces, order, integrals, first, rows, each=2):
+def product(pieces, order, integrals, each=4):
     slots, tile, width = integrals.shape
-    count, groups, cols = len(pieces), Y * Z, tile // (X * C)
+    count = len(pieces)
+    groups, _, rows, cols = pieces[0][0].shape
     halves = tuple(i for i, piece in enumerate(pieces) if len(piece) == 2)
     arrays = [a for piece in pieces for a in piece]
     m, k = groups * rows, slots * tile
     steps = count // each
     deep = each * slots * cols
     return pl.pallas_call(
-        functools.partial(product_kernel, first, halves),
+        functools.partial(product_kernel, halves),
         out_shape=jax.ShapeDtypeStruct((groups, width // 128 * rows + 8, 128), jnp.float32),
         in_specs=[pl.BlockSpec(memory_space=pltpu.SMEM)] + [pl.BlockSpec(memory_space=pl.ANY)] * (len(arrays) + 1),
         out_specs=pl.BlockSpec(memory_space=pltpu.VMEM),
@@ -120,8 +121,8 @@
         ],
         compiler_params=pltpu.CompilerParams(vmem_limit_bytes=PRODUCT_VMEM),
         cost_estimate=pl.CostEstimate(
-            flops=2 * m * k * width // COST_DIV,
-            bytes_accessed=(2 * (m * k + k * width) + 4 * m * width) // COST_DIV,
+            flops=2 * m * k * width,
+            bytes_accessed=2 * (m * k + k * width) + 4 * m * width,
             transcendentals=0,
         ),
         name="product",
@@ -139,7 +140,7 @@
 
 
 def after(a, *others):
-    return lax.optimization_barrier((a, *others))[0]
+    return lax.optimization_barrier((a, *others))[0] if others else a
 
 
 def swap(a):
@@ -149,32 +150,32 @@
 def on_device(t2, keep, integrals):
     slots = integrals.shape[0]
     mx, mc = lax.axis_index("x"), lax.axis_index("c")
-    packed = pack(t2, keep, Y * Z, slots, [sum(g) for g in GROUPS])
+    packed = pack(t2, keep, Y * Z, slots, GROUPS)
     places = [((mx + d) % X) * C + c for c in (mc, 1 - mc) for d in (0, -1, 1, 2)]
     order = jnp.stack(places).astype(jnp.int32)
 
-    results, sides, last, before = [], [], [], []
-    for part, group in zip(packed, GROUPS):
-        own = lax.all_to_all(part, ("y", "z"), split_axis=0, concat_axis=0, tiled=True)
-        own = after(own, *sides) if sides else own
+    owns = []
+    for part in packed:
+        part = after(part, *owns[-1:])
+        owns.append(lax.all_to_all(part, ("y", "z"), split_axis=0, concat_axis=0, tiled=True))
+    results, earlier, last, before = [], [], [], []
+    for i, own in enumerate(owns):
+        own = after(own, *earlier)
         left, right = shift(own, "x", 1), shift(own, "x", -1)
-        sides = [left, right]
-        near = [own, left, right]
-        across = [swap(after(a, *last)) for a in near]
-        first = 0
         half = own.shape[0] // 2
-        for rows in group:
-            span = slice(first, first + rows)
-            far = [shift(left[:half, :, span], "x", 1), shift(right[half:, :, span], "x", -1)]
-            far_across = [swap(after(a, *last)) for a in far]
-            pieces = [[a] for a in near] + [far] + [[a] for a in across] + [far_across]
-            blocks = product(pieces, order, integrals, first, rows)
-            sent = blocks.astype(jnp.float16)
-            last = [sent]
-            got, total = add_over_owners(after(sent, *before) if before else sent)
-            before = [got]
-            results.append(total)
-            first += rows
+        halves = [after(a, *owns[i + 1 : i + 2]) for a in (left[:half], right[half:])]
+        far = [shift(halves[0], "x", 1), shift(halves[1], "x", -1)]
+        earlier = far if BY_FAR else [left, right]
+        mine = [[own], [left], [right], far]
+        near_held = [] if NEAR_FREE else last
+        theirs = [[swap(after(a, *near_held)) for a in piece] for piece in mine[:3]]
+        theirs.append([swap(after(a, *last)) for a in far])
+        blocks = product(mine + theirs, order, integrals)
+        sent = blocks.astype(jnp.float16)
+        last = [sent]
+        got, total = add_over_owners(after(sent, *before))
+        before = [got]
+        results.append(total)
     return (0.5 * jnp.concatenate(results, axis=0)).astype(jnp.bfloat16)
 
 

time: 186 us -> 177 us (0.952)
  Pallas kernels: 40.2 us -> 31 us
  starting transfers between devices: 35.6 us -> 29.4 us
  waiting for transfers between devices: 70 us -> 73.6 us
  local copies, waits for them, and re-layouts: 7 us -> 10.1 us
  blocking collectives: 22.3 us -> 25 us
  other arithmetic: 9.94 us -> 7.26 us
    all_to_all x3 -> x2, waiting for transfers between devices: 14.4 us -> 28.7 us  [add_over_owners(): lax.all_to_all(sent, ('y', 'z'), split_axis=0, concat_axis=0, tiled=True)]
    ppermute x22 -> x18, waiting for transfers between devices: 55.5 us -> 44.9 us  [shift(): return lax.ppermute(a, axis, [(i, (i + by) % n) for i in range(n)])]
    pallas_call x3 -> x2, Pallas kernels: 36.6 us -> 27.5 us  [product(): pl.pallas_call(functools.partial(product_kernel, halves), out_shape=jax.S...]
    all_to_all x3 -> x2, starting transfers between devices: 18.1 us -> 13.5 us  [add_over_owners(): lax.all_to_all(sent, ('y', 'z'), split_axis=0, concat_axis=0, tiled=True)]
    unnamed x4 -> x12, local copies, waits for them, and re-layouts: 2.01 us -> 5.94 us
    all_to_all x1, blocking collectives: 22.3 us -> 25 us  [on_device(): lax.all_to_all(part, ('y', 'z'), split_axis=0, concat_axis=0, tiled=True)]
    ppermute x22 -> x18, starting transfers between devices: 13.8 us -> 12.1 us  [shift(): return lax.ppermute(a, axis, [(i, (i + by) % n) for i in range(n)])]
    slice x6 -> x4, local copies, waits for them, and re-layouts: 4.87 us -> 4.07 us  [on_device(): halves = [after(a, *owns[i + 1:i + 2]) for a in (left[:half], right[half:])]]
  transfers between devices with their start and end apart: 26 -> 21, of which waited for: 15 -> 8; matrix products, arithmetic and copies ran while one was open for 8% -> 6% of each run, Pallas kernels for 20% -> 16%
where the time goes in v3:
time: 177 us
  waiting for transfers between devices  73.6 us (42%)
  Pallas kernels  31 us (18%)
  starting transfers between devices  29.4 us (17%)
  blocking collectives  25 us (14%)
  local copies, waits for them, and re-layouts  10.1 us (6%)
  other arithmetic  7.26 us (4%)
    ppermute x18, waiting for transfers between devices, shift(): return lax.ppermute(a, axis, [(i, (i + by) % n) for i in range(n)])  44.9 us
    all_to_all x2, waiting for transfers between devices, add_over_owners(): lax.all_to_all(sent, ('y', 'z'), split_axis=0, concat_axis=0, tiled=True)  28.7 us
    pallas_call x2, Pallas kernels, product(): pl.pallas_call(functools.partial(product_kernel, halves), out_shape=jax.S...  27.5 us
    all_to_all x1, blocking collectives, on_device(): lax.all_to_all(part, ('y', 'z'), split_axis=0, concat_axis=0, tiled=True)  25 us
    all_to_all x2, starting transfers between devices, add_over_owners(): lax.all_to_all(sent, ('y', 'z'), split_axis=0, concat_axis=0, tiled=True)  13.5 us
    ppermute x18, starting transfers between devices, shift(): return lax.ppermute(a, axis, [(i, (i + by) % n) for i in range(n)])  12.1 us
    unnamed x12, local copies, waits for them, and re-layouts  5.94 us
    slice x4, local copies, waits for them, and re-layouts, on_device(): halves = [after(a, *owns[i + 1:i + 2]) for a in (left[:half], right[half:])]  4.07 us
  transfers between devices with their start and end apart: 21, of which 8 were waited for; matrix products, arithmetic and copies ran while one was open for 6% of the time, Pallas kernels for 16%

profile of v3, /device:TPU:0, one launch (start us, length us, event | category | flops | bytes accessed | tf_op | source)
XLA Modules:
  0.0 176.6 jit_solution(7353086815186309368)
XLA Ops:
  0.0 3.5 %pack.1 = (bf16[16,4,64,128]{3,2,1,0:T(8,128)(2,1)}, bf16[16,4,64,128]{3,2,1,0:T(8,128)(2,1)}) custom-call(s32[40]{0:T(128)} %keep_ref.1, bf16[128,40,128]{2,1,0:T(8,128)(2,1)} %t2_ref.1), custom_call_target="tpu_custom_call" | custom-call | tf_op jit(solution)/shard_map/pack/pallas_call | solution.py:44
  3.5 25.0 %all_to_all.20.refs_0_ = bf16[16,4,64,128]{3,2,1,0:T(8,128)(2,1)S(1)} all-to-all(bf16[16,4,64,128]{3,2,1,0:T(8,128)(2,1)} %get-tuple-element.14), channel_id=1, replica_groups=mesh['x'=4,'c'=2,'y'=4,'z'=4] {'y','z'}, dimensions={0} | all-to-all | bytes 2097152 | tf_op jit(solution)/shard_map/all_to_all | solution.py:160
  28.5 2.8 %collective-permute-start.1 = (bf16[16,4,64,128]{3,2,1,0:T(8,128)(2,1)S(1)}, bf16[16,4,64,128]{3,2,1,0:T(8,128)(2,1)}, u32[]{:S(2)}, u32[]{:S(2)}) collective-permute-start(bf16[16,4,64,128]{3,2,1,0:T(8,128)(2,1)S(1)} %all_to_all.20.refs_0_), channel_id=1, source_target_pairs={{0,96},{32,0},{64,32},{96,64},{1,97},{33,1},{65,33},{97,65},{2,98}... | collective-permute-start | bytes 3145736 | tf_op jit(solution)/shard_map/ppermute | solution.py:22
  31.3 3.8 %all-to-all-start.1 = ((bf16[16,4,64,128]{3,2,1,0:T(8,128)(2,1)}), bf16[16,4,64,128]{3,2,1,0:T(8,128)(2,1)S(1)}, u32[]{:S(2)}, u32[]{:S(2)}) async-start(bf16[16,4,64,128]{3,2,1,0:T(8,128)(2,1)} %get-tuple-element.16), calls=%async_computation.1 | async-start | bytes 2097152 | tf_op jit(solution)/shard_map/all_to_all | solution.py:160
  35.3 17.1 %collective-permute-done.1.refs_2_ = bf16[16,4,64,128]{3,2,1,0:T(8,128)(2,1)} collective-permute-done((bf16[16,4,64,128]{3,2,1,0:T(8,128)(2,1)S(1)}, bf16[16,4,64,128]{3,2,1,0:T(8,128)(2,1)}, u32[]{:S(2)}, u32[]{:S(2)}) %collective-permute-start.1) | collective-permute-done | bytes 1048608 | tf_op jit(solution)/shard_map/ppermute | solution.py:22
  52.4 1.9 %slice.33 = bf16[8,4,64,128]{3,2,1,0:T(8,128)(2,1)} slice(bf16[16,4,64,128]{3,2,1,0:T(8,128)(2,1)} %collective-permute-done.1.refs_2_), slice={[8:16], [0:4], [0:64], [0:128]} | slice | bytes 1048576 | tf_op jit(solution)/shard_map/slice | solution.py:166
  54.3 3.8 %collective-permute-start.3 = (bf16[8,4,64,128]{3,2,1,0:T(8,128)(2,1)}, bf16[8,4,64,128]{3,2,1,0:T(8,128)(2,1)S(1)}, u32[]{:S(2)}, u32[]{:S(2)}) collective-permute-start(bf16[8,4,64,128]{3,2,1,0:T(8,128)(2,1)} %slice.33), channel_id=1, source_target_pairs={{0,96},{32,0},{64,32},{96,64},{1,97},{33,1},{65,33},{97,65},{2,98}... | collective-permute-start | bytes 1572872 | tf_op jit(solution)/shard_map/ppermute | solution.py:22
  58.1 1.6 collective-permute-done.refs_1_
  59.7 1.1 slice.32
  61.4 6.0 %collective-permute-done.3.refs_4_ = bf16[8,4,64,128]{3,2,1,0:T(8,128)(2,1)S(1)} collective-permute-done((bf16[8,4,64,128]{3,2,1,0:T(8,128)(2,1)}, bf16[8,4,64,128]{3,2,1,0:T(8,128)(2,1)S(1)}, u32[]{:S(2)}, u32[]{:S(2)}) %collective-permute-start.3) | collective-permute-done | bytes 524320 | tf_op jit(solution)/shard_map/ppermute | solution.py:22
  67.4 0.8 copy-done.2
  68.2 4.9 %collective-permute-done.2.refs_3_ = bf16[8,4,64,128]{3,2,1,0:T(8,128)(2,1)} collective-permute-done((bf16[8,4,64,128]{3,2,1,0:T(8,128)(2,1)S(1)}, bf16[8,4,64,128]{3,2,1,0:T(8,128)(2,1)}, u32[]{:S(2)}, u32[]{:S(2)}) %collective-permute-start.2) | collective-permute-done | bytes 524320 | tf_op jit(solution)/shard_map/ppermute | solution.py:22
  73.2 1.0 copy-done
  74.2 0.9 copy-done.4
  75.0 2.0 %collective-permute-start.9 = (bf16[16,4,64,128]{3,2,1,0:T(8,128)(2,1)S(1)}, bf16[16,4,64,128]{3,2,1,0:T(8,128)(2,1)}, u32[]{:S(2)}, u32[]{:S(2)}) collective-permute-start(bf16[16,4,64,128]{3,2,1,0:T(8,128)(2,1)S(1)} %all-to-all-done.1.refs_0_), channel_id=1, source_target_pairs={{0,32},{32,64},{64,96},{96,0},{1,33},{33,65},{65,97},{97,1},{2,34}... | collective-permute-start | bytes 3145736 | tf_op jit(solution)/shard_map/ppermute | solution.py:22
  77.2 1.2 copy-done.1
  78.4 1.0 copy-done.3
  79.4 1.0 copy-done.5
  80.5 14.0 %product.2 = f32[16,520,128]{2,1,0:T(8,128)S(1)} custom-call(s32[8]{0:T(128)S(1)} %stack.35.order_ref, bf16[16,4,64,128]{3,2,1,0:T(8,128)(2,1)S(1)} %all_to_all.20.refs_0_, bf16[16,4,64,128]{3,2,1,0:T(8,128)(2,1)} %collective-permute-done.refs_1_, bf16[16,4,64,128]{3,2,1,0:T(8,128)(2,1)} %collective-permute-done.1.refs_2_, ...), custom_call_target="tpu_custom_call" | custom-call | flops 8589934592 | bytes 20971520 | tf_op jit(solution)/shard_map/product/pallas_call | solution.py:111
  94.4 1.6 convert_element_type.23
  96.0 6.6 %all-to-all-start.2 = ((f16[16,520,128]{2,1,0:T(8,128)(2,1)}), f16[16,520,128]{2,1,0:T(8,128)(2,1)}, u32[]{:S(2)}, u32[]{:S(2)}) async-start(f16[16,520,128]{2,1,0:T(8,128)(2,1)} %convert_element_type.23), calls=%async_computation.2 | async-start | bytes 4259840 | tf_op jit(solution)/shard_map/all_to_all | solution.py:136
  102.7 1.3 collective-permute-start.12
  104.0 1.1 slice.36
  105.1 0.9 collective-permute-start.11
  106.4 9.8 %collective-permute-done.12.refs_4_ = bf16[8,4,64,128]{3,2,1,0:T(8,128)(2,1)S(1)} collective-permute-done((bf16[8,4,64,128]{3,2,1,0:T(8,128)(2,1)S(1)}, bf16[8,4,64,128]{3,2,1,0:T(8,128)(2,1)S(1)}, u32[]{:S(2)}, u32[]{:S(2)}) %collective-permute-start.12) | collective-permute-done | bytes 524320 | tf_op jit(solution)/shard_map/ppermute | solution.py:22
  116.3 3.6 %collective-permute-done.11.refs_3_ = bf16[8,4,64,128]{3,2,1,0:T(8,128)(2,1)S(1)} collective-permute-done((bf16[8,4,64,128]{3,2,1,0:T(8,128)(2,1)S(1)}, bf16[8,4,64,128]{3,2,1,0:T(8,128)(2,1)S(1)}, u32[]{:S(2)}, u32[]{:S(2)}) %collective-permute-start.11) | collective-permute-done | bytes 524320 | tf_op jit(solution)/shard_map/ppermute | solution.py:22
  119.8 1.9 %collective-permute-done.16.refs_8_ = bf16[8,4,64,128]{3,2,1,0:T(8,128)(2,1)S(1)} collective-permute-done((bf16[8,4,64,128]{3,2,1,0:T(8,128)(2,1)S(1)}, bf16[8,4,64,128]{3,2,1,0:T(8,128)(2,1)S(1)}, u32[]{:S(2)}, u32[]{:S(2)}) %collective-permute-start.16) | collective-permute-done | bytes 524320 | tf_op jit(solution)/shard_map/ppermute | solution.py:22
  121.7 13.5 %product.3 = f32[16,520,128]{2,1,0:T(8,128)S(1)} custom-call(s32[8]{0:T(128)S(1)} %stack.35.order_ref, bf16[16,4,64,128]{3,2,1,0:T(8,128)(2,1)S(1)} %all-to-all-done.1.refs_0_, bf16[16,4,64,128]{3,2,1,0:T(8,128)(2,1)} %collective-permute-done.9.refs_1_, bf16[16,4,64,128]{3,2,1,0:T(8,128)(2,1)S(1)} %collective-permute-done.10.refs_2_, ...), custom_call_target="tpu_custom_call" | custom-call | flops 8589934592 | bytes 20971520 | tf_op jit(solution)/shard_map/product/pallas_call | solution.py:111
  135.3 1.7 convert_element_type.26
  136.9 6.9 %all-to-all-start.3 = ((f16[16,520,128]{2,1,0:T(8,128)(2,1)}), f16[16,520,128]{2,1,0:T(8,128)(2,1)S(1)}, u32[]{:S(2)}, u32[]{:S(2)}) async-start(f16[16,520,128]{2,1,0:T(8,128)(2,1)} %convert_element_type.26), calls=%async_computation.3 | async-start | bytes 4259840 | tf_op jit(solution)/shard_map/all_to_all | solution.py:136
  144.6 2.0 %multiply_reduce_fusion.1 = f32[512,128]{1,0:T(8,128)S(1)} fusion(f16[16,520,128]{2,1,0:T(8,128)(2,1)} %all-to-all-done.2, f32[16,128]{1,0:T(8,128)S(1)} %bitcast.28), kind=kLoop, calls=%fused_computation.1 | loop fusion | flops 3080192 | bytes 2367488 | tf_op jit(solution)/shard_map/reduce_sum | solution.py:138
  146.7 28.7 %all-to-all-done.3 = f16[16,520,128]{2,1,0:T(8,128)(2,1)S(1)} async-done(((f16[16,520,128]{2,1,0:T(8,128)(2,1)}), f16[16,520,128]{2,1,0:T(8,128)(2,1)S(1)}, u32[]{:S(2)}, u32[]{:S(2)}) %all-to-all-start.3) | async-done | bytes 2129952 | tf_op jit(solution)/shard_map/all_to_all | solution.py:136
  (40 shorter events, 3.5 us)
Async XLA Ops:
  28.5 23.9 %collective-permute-start.1 = (bf16[16,4,64,128]{3,2,1,0:T(8,128)(2,1)S(1)}, bf16[16,4,64,128]{3,2,1,0:T(8,128)(2,1)}, u32[]{:S(2)}, u32[]{:S(2)}) collective-permute-start(bf16[16,4,64,128]{3,2,1,0:T(8,128)(2,1)S(1)} %all_to_all.20.refs_0_), channel_id=1, source_target_pairs={{0,96},{32,0},{64,32},{96,64},{1,97},{33,1},{65,33},{97,65},{2,98}... | collective-permute-start | bytes 3145736 | tf_op jit(solution)/shard_map/ppermute | solution.py:22
  31.3 23.0 %all-to-all-start.1 = ((bf16[16,4,64,128]{3,2,1,0:T(8,128)(2,1)}), bf16[16,4,64,128]{3,2,1,0:T(8,128)(2,1)S(1)}, u32[]{:S(2)}, u32[]{:S(2)}) async-start(bf16[16,4,64,128]{3,2,1,0:T(8,128)(2,1)} %get-tuple-element.16), calls=%async_computation.1 | async-start | bytes 2097152 | tf_op jit(solution)/shard_map/all_to_all | solution.py:160
  35.1 24.6 %collective-permute-start = (bf16[16,4,64,128]{3,2,1,0:T(8,128)(2,1)S(1)}, bf16[16,4,64,128]{3,2,1,0:T(8,128)(2,1)}, u32[]{:S(2)}, u32[]{:S(2)}) collective-permute-start(bf16[16,4,64,128]{3,2,1,0:T(8,128)(2,1)S(1)} %all_to_all.20.refs_0_), channel_id=1, source_target_pairs={{0,32},{32,64},{64,96},{96,0},{1,33},{33,65},{65,97},{97,1},{2,34}... | collective-permute-start | bytes 3145736 | tf_op jit(solution)/shard_map/ppermute | solution.py:22
  35.2 38.0 %collective-permute-start.4 = (bf16[16,4,64,128]{3,2,1,0:T(8,128)(2,1)S(1)}, bf16[16,4,64,128]{3,2,1,0:T(8,128)(2,1)S(1)}, u32[]{:S(2)}, u32[]{:S(2)}) collective-permute-start(bf16[16,4,64,128]{3,2,1,0:T(8,128)(2,1)S(1)} %all_to_all.20.refs_0_), channel_id=1, source_target_pairs={{0,16},{16,0},{1,17},{17,1},{2,18},{18,2},{3,19},{19,3},{4,20},{20... | collective-permute-start | bytes 3145736 | tf_op jit(solution)/shard_map/ppermute | solution.py:22
  54.3 13.1 %collective-permute-start.3 = (bf16[8,4,64,128]{3,2,1,0:T(8,128)(2,1)}, bf16[8,4,64,128]{3,2,1,0:T(8,128)(2,1)S(1)}, u32[]{:S(2)}, u32[]{:S(2)}) collective-permute-start(bf16[8,4,64,128]{3,2,1,0:T(8,128)(2,1)} %slice.33), channel_id=1, source_target_pairs={{0,96},{32,0},{64,32},{96,64},{1,97},{33,1},{65,33},{97,65},{2,98}... | collective-permute-start | bytes 1572872 | tf_op jit(solution)/shard_map/ppermute | solution.py:22
  60.8 12.4 %collective-permute-start.2 = (bf16[8,4,64,128]{3,2,1,0:T(8,128)(2,1)S(1)}, bf16[8,4,64,128]{3,2,1,0:T(8,128)(2,1)}, u32[]{:S(2)}, u32[]{:S(2)}) collective-permute-start(bf16[8,4,64,128]{3,2,1,0:T(8,128)(2,1)S(1)} %slice.32), channel_id=1, source_target_pairs={{0,32},{32,64},{64,96},{96,0},{1,33},{33,65},{65,97},{97,1},{2,34}... | collective-permute-start | bytes 1572872 | tf_op jit(solution)/shard_map/ppermute | solution.py:22
  60.8 16.3 %collective-permute-start.5 = (bf16[16,4,64,128]{3,2,1,0:T(8,128)(2,1)}, bf16[16,4,64,128]{3,2,1,0:T(8,128)(2,1)}, u32[]{:S(2)}, u32[]{:S(2)}) collective-permute-start(bf16[16,4,64,128]{3,2,1,0:T(8,128)(2,1)} %collective-permute-done.refs_1_), channel_id=1, source_target_pairs={{0,16},{16,0},{1,17},{17,1},{2,18},{18,2},{3,19},{19,3},{4,20},{20... | collective-permute-start | bytes 3145736 | tf_op jit(solution)/shard_map/ppermute | solution.py:22
  60.9 16.2 %collective-permute-start.6 = (bf16[16,4,64,128]{3,2,1,0:T(8,128)(2,1)}, bf16[16,4,64,128]{3,2,1,0:T(8,128)(2,1)}, u32[]{:S(2)}, u32[]{:S(2)}) collective-permute-start(bf16[16,4,64,128]{3,2,1,0:T(8,128)(2,1)} %collective-permute-done.1.refs_2_), channel_id=1, source_target_pairs={{0,16},{16,0},{1,17},{17,1},{2,18},{18,2},{3,19},{19,3},{4,20},{20... | collective-permute-start | bytes 3145736 | tf_op jit(solution)/shard_map/ppermute | solution.py:22
  67.4 6.7 %collective-permute-start.8 = (bf16[8,4,64,128]{3,2,1,0:T(8,128)(2,1)S(1)}, bf16[8,4,64,128]{3,2,1,0:T(8,128)(2,1)S(1)}, u32[]{:S(2)}, u32[]{:S(2)}) collective-permute-start(bf16[8,4,64,128]{3,2,1,0:T(8,128)(2,1)S(1)} %collective-permute-done.3.refs_4_), channel_id=1, source_target_pairs={{0,16},{16,0},{1,17},{17,1},{2,18},{18,2},{3,19},{19,3},{4,20},{20... | collective-permute-start | bytes 1572872 | tf_op jit(solution)/shard_map/ppermute | solution.py:22
  67.4 0.8 copy-start.2
  73.2 4.0 %collective-permute-start.7 = (bf16[8,4,64,128]{3,2,1,0:T(8,128)(2,1)}, bf16[8,4,64,128]{3,2,1,0:T(8,128)(2,1)}, u32[]{:S(2)}, u32[]{:S(2)}) collective-permute-start(bf16[8,4,64,128]{3,2,1,0:T(8,128)(2,1)} %collective-permute-done.2.refs_3_), channel_id=1, source_target_pairs={{0,16},{16,0},{1,17},{17,1},{2,18},{18,2},{3,19},{19,3},{4,20},{20... | collective-permute-start | bytes 1572872 | tf_op jit(solution)/shard_map/ppermute | solution.py:22
  73.2 1.0 copy-start
  74.2 28.5 %collective-permute-start.10 = (bf16[16,4,64,128]{3,2,1,0:T(8,128)(2,1)S(1)}, bf16[16,4,64,128]{3,2,1,0:T(8,128)(2,1)S(1)}, u32[]{:S(2)}, u32[]{:S(2)}) collective-permute-start(bf16[16,4,64,128]{3,2,1,0:T(8,128)(2,1)S(1)} %all-to-all-done.1.refs_0_), channel_id=1, source_target_pairs={{0,96},{32,0},{64,32},{96,64},{1,97},{33,1},{65,33},{97,65},{2,98}... | collective-permute-start | bytes 3145736 | tf_op jit(solution)/shard_map/ppermute | solution.py:22
  74.2 0.9 copy-start.4
  75.0 29.0 %collective-permute-start.9 = (bf16[16,4,64,128]{3,2,1,0:T(8,128)(2,1)S(1)}, bf16[16,4,64,128]{3,2,1,0:T(8,128)(2,1)}, u32[]{:S(2)}, u32[]{:S(2)}) collective-permute-start(bf16[16,4,64,128]{3,2,1,0:T(8,128)(2,1)S(1)} %all-to-all-done.1.refs_0_), channel_id=1, source_target_pairs={{0,32},{32,64},{64,96},{96,0},{1,33},{33,65},{65,97},{97,1},{2,34}... | collective-permute-start | bytes 3145736 | tf_op jit(solution)/shard_map/ppermute | solution.py:22
  77.1 1.2 copy-start.1
  78.4 1.0 copy-start.3
  79.4 1.0 copy-start.5
  96.0 40.9 %all-to-all-start.2 = ((f16[16,520,128]{2,1,0:T(8,128)(2,1)}), f16[16,520,128]{2,1,0:T(8,128)(2,1)}, u32[]{:S(2)}, u32[]{:S(2)}) async-start(f16[16,520,128]{2,1,0:T(8,128)(2,1)} %convert_element_type.23), calls=%async_computation.2 | async-start | bytes 4259840 | tf_op jit(solution)/shard_map/all_to_all | solution.py:136
  102.7 13.6 %collective-permute-start.12 = (bf16[8,4,64,128]{3,2,1,0:T(8,128)(2,1)S(1)}, bf16[8,4,64,128]{3,2,1,0:T(8,128)(2,1)S(1)}, u32[]{:S(2)}, u32[]{:S(2)}) collective-permute-start(bf16[8,4,64,128]{3,2,1,0:T(8,128)(2,1)S(1)} %slice.37), channel_id=1, source_target_pairs={{0,96},{32,0},{64,32},{96,64},{1,97},{33,1},{65,33},{97,65},{2,98}... | collective-permute-start | bytes 1572872 | tf_op jit(solution)/shard_map/ppermute | solution.py:22
  105.1 14.8 %collective-permute-start.11 = (bf16[8,4,64,128]{3,2,1,0:T(8,128)(2,1)S(1)}, bf16[8,4,64,128]{3,2,1,0:T(8,128)(2,1)S(1)}, u32[]{:S(2)}, u32[]{:S(2)}) collective-permute-start(bf16[8,4,64,128]{3,2,1,0:T(8,128)(2,1)S(1)} %slice.36), channel_id=1, source_target_pairs={{0,32},{32,64},{64,96},{96,0},{1,33},{33,65},{65,97},{97,1},{2,34}... | collective-permute-start | bytes 1572872 | tf_op jit(solution)/shard_map/ppermute | solution.py:22
  105.9 13.9 %collective-permute-start.13 = (bf16[16,4,64,128]{3,2,1,0:T(8,128)(2,1)S(1)}, bf16[16,4,64,128]{3,2,1,0:T(8,128)(2,1)S(1)}, u32[]{:S(2)}, u32[]{:S(2)}) collective-permute-start(bf16[16,4,64,128]{3,2,1,0:T(8,128)(2,1)S(1)} %all-to-all-done.1.refs_0_), channel_id=1, source_target_pairs={{0,16},{16,0},{1,17},{17,1},{2,18},{18,2},{3,19},{19,3},{4,20},{20... | collective-permute-start | bytes 3145736 | tf_op jit(solution)/shard_map/ppermute | solution.py:22
  105.9 15.8 %collective-permute-start.14 = (bf16[16,4,64,128]{3,2,1,0:T(8,128)(2,1)}, bf16[16,4,64,128]{3,2,1,0:T(8,128)(2,1)S(1)}, u32[]{:S(2)}, u32[]{:S(2)}) collective-permute-start(bf16[16,4,64,128]{3,2,1,0:T(8,128)(2,1)} %collective-permute-done.9.refs_1_), channel_id=1, source_target_pairs={{0,16},{16,0},{1,17},{17,1},{2,18},{18,2},{3,19},{19,3},{4,20},{20... | collective-permute-start | bytes 3145736 | tf_op jit(solution)/shard_map/ppermute | solution.py:22
  106.4 15.3 %collective-permute-start.15 = (bf16[16,4,64,128]{3,2,1,0:T(8,128)(2,1)S(1)}, bf16[16,4,64,128]{3,2,1,0:T(8,128)(2,1)S(1)}, u32[]{:S(2)}, u32[]{:S(2)}) collective-permute-start(bf16[16,4,64,128]{3,2,1,0:T(8,128)(2,1)S(1)} %collective-permute-done.10.refs_2_), channel_id=1, source_target_pairs={{0,16},{16,0},{1,17},{17,1},{2,18},{18,2},{3,19},{19,3},{4,20},{20... | collective-permute-start | bytes 3145736 | tf_op jit(solution)/shard_map/ppermute | solution.py:22
  116.2 3.6 %collective-permute-start.17 = (bf16[8,4,64,128]{3,2,1,0:T(8,128)(2,1)S(1)}, bf16[8,4,64,128]{3,2,1,0:T(8,128)(2,1)S(1)}, u32[]{:S(2)}, u32[]{:S(2)}) collective-permute-start(bf16[8,4,64,128]{3,2,1,0:T(8,128)(2,1)S(1)} %collective-permute-done.12.refs_4_), channel_id=1, source_target_pairs={{0,16},{16,0},{1,17},{17,1},{2,18},{18,2},{3,19},{19,3},{4,20},{20... | collective-permute-start | bytes 1572872 | tf_op jit(solution)/shard_map/ppermute | solution.py:22
  119.8 1.9 %collective-permute-start.16 = (bf16[8,4,64,128]{3,2,1,0:T(8,128)(2,1)S(1)}, bf16[8,4,64,128]{3,2,1,0:T(8,128)(2,1)S(1)}, u32[]{:S(2)}, u32[]{:S(2)}) collective-permute-start(bf16[8,4,64,128]{3,2,1,0:T(8,128)(2,1)S(1)} %collective-permute-done.11.refs_3_), channel_id=1, source_target_pairs={{0,16},{16,0},{1,17},{17,1},{2,18},{18,2},{3,19},{19,3},{4,20},{20... | collective-permute-start | bytes 1572872 | tf_op jit(solution)/shard_map/ppermute | solution.py:22
  136.9 38.4 %all-to-all-start.3 = ((f16[16,520,128]{2,1,0:T(8,128)(2,1)}), f16[16,520,128]{2,1,0:T(8,128)(2,1)S(1)}, u32[]{:S(2)}, u32[]{:S(2)}) async-start(f16[16,520,128]{2,1,0:T(8,128)(2,1)} %convert_element_type.26), calls=%async_computation.3 | async-start | bytes 4259840 | tf_op jit(solution)/shard_map/all_to_all | solution.py:136

commit v4 on v3

--- a/solution.py
+++ b/solution.py
@@ -9,10 +9,7 @@
 from jax.sharding import PartitionSpec as P
 
 X, C, Y, Z = 4, 2, 4, 4
-GROUPS = (64, 64)
-BY_FAR = True
-NEAR_FREE = True
-COLUMN_BLOCKS = 8
+GROUPS = ((64,), (64,))
 STEP = 512
 VMEM_LIMIT = 56 * 1024 * 1024
 PRODUCT_VMEM = 40 * 1024 * 1024
@@ -52,8 +49,8 @@
     )(keep, t2)
 
 
-def product_kernel(halves, order_ref, *refs):
-    arrays, (b_ref, out_ref, a_in, b_in, acc, sems) = list(refs[:-6]), refs[-6:]
+def product_kernel(plan, order_ref, *refs):
+    arrays, (b_ref, out_ref, a_in, b_in, acc, sems) = refs[:-6], refs[-6:]
     count, groups, slots, rows, cols = a_in.shape
     steps, deep, width = b_in.shape
     each = count // steps
@@ -65,10 +62,11 @@
             span = pl.ds((u * slots + s) * cols, cols)
             at = pl.multiple_of(order_ref[i] * cols, cols)
             now.append(pltpu.make_async_copy(b_ref.at[s, pl.ds(at, cols), :], b_in.at[t, span, :], sems.at[i, s]))
-        got = [arrays.pop(0)] if i not in halves else [arrays.pop(0), arrays.pop(0)]
-        some = groups // len(got)
-        for h, array in enumerate(got):
-            now.append(pltpu.make_async_copy(array, a_in.at[i, pl.ds(h * some, some)], sems.at[i, slots + h]))
+        some = groups // len(plan[i])
+        for h, (which, lead, first) in enumerate(plan[i]):
+            source = arrays[which] if lead is None else arrays[which].at[lead]
+            source = source.at[:, :, pl.ds(first, rows), :]
+            now.append(pltpu.make_async_copy(source, a_in.at[i, pl.ds(h * some, some)], sems.at[i, slots + h]))
         for copy in now:
             copy.start()
         copies.append(now)
@@ -93,24 +91,23 @@
         most = lax.fori_loop(0, width // STEP, some_columns, jnp.zeros((1, 1), jnp.float32))
     up = 13 - jnp.floor(jnp.log2(jnp.broadcast_to(jnp.maximum(most, 2.0**-100), (8, 128))))
     scale = jnp.exp2(up)[:1]
-    for n in range(width // 128):
+    per = width // 256
+    for n in range(2 * per):
         part = acc[:, n * 128 : (n + 1) * 128] * scale
-        out_ref[:, n * rows : (n + 1) * rows, :] = part.reshape(groups, rows, 128)
-    out_ref[:, width // 128 * rows :, :] = jnp.broadcast_to(up[None], (groups, 8, 128))
-
-
-def product(pieces, order, integrals, each=4):
+        out_ref[:, n // per, pl.ds(n % per * rows, rows), :] = part.reshape(groups, rows, 128)
+    for h in range(2):
+        out_ref[:, h, pl.ds(per * rows, 8), :] = jnp.broadcast_to(up[None], (groups, 8, 128))
+
+
+def product(arrays, plan, rows, order, integrals, each=4):
     slots, tile, width = integrals.shape
-    count = len(pieces)
-    groups, _, rows, cols = pieces[0][0].shape
-    halves = tuple(i for i, piece in enumerate(pieces) if len(piece) == 2)
-    arrays = [a for piece in pieces for a in piece]
+    count, groups, cols = len(plan), Y * Z, arrays[0].shape[-1]
     m, k = groups * rows, slots * tile
     steps = count // each
     deep = each * slots * cols
     return pl.pallas_call(
-        functools.partial(product_kernel, halves),
-        out_shape=jax.ShapeDtypeStruct((groups, width // 128 * rows + 8, 128), jnp.float32),
+        functools.partial(product_kernel, plan),
+        out_shape=jax.ShapeDtypeStruct((groups, 2, width // 256 * rows + 8, 128), jnp.float32),
         in_specs=[pl.BlockSpec(memory_space=pltpu.SMEM)] + [pl.BlockSpec(memory_space=pl.ANY)] * (len(arrays) + 1),
         out_specs=pl.BlockSpec(memory_space=pltpu.VMEM),
         scratch_shapes=[
@@ -129,14 +126,21 @@
     )(order, *arrays, integrals)
 
 
-def add_over_owners(sent):
-    n = COLUMN_BLOCKS
-    body = sent.shape[1] - 8
-    rows = body // n
+def unscaled(blocks):
+    n = blocks.shape[-2] - 8
+    up = blocks[..., n : n + 1, :].astype(jnp.float32)
+    return blocks[..., :n, :].astype(jnp.float32) * jnp.exp2(-up)
+
+
+def at_once(blocks, *before):
+    sent = after(blocks.astype(jnp.float16), *before)
     got = lax.all_to_all(sent, ("y", "z"), split_axis=0, concat_axis=0, tiled=True)
-    back = jnp.exp2(-got[:, body, :].astype(jnp.float32))
-    total = jnp.sum(got[:, :body].astype(jnp.float32) * back[:, None, :], axis=0)
-    return got, jnp.swapaxes(total.reshape(n, rows, 128), 0, 1).reshape(rows, n * 128)
+    return sent, got, jnp.sum(unscaled(got), axis=0)
+
+
+def as_rows(total, rows):
+    n = total.shape[0] * total.shape[1] // rows
+    return jnp.swapaxes(total.reshape(n, rows, 128), 0, 1).reshape(rows, n * 128)
 
 
 def after(a, *others):
@@ -145,12 +149,31 @@
 
 def swap(a):
     return shift(a, "c", 1, 2)
+
+
+def near_pieces(own):
+    return [own, shift(own, "x", 1), shift(own, "x", -1)]
+
+
+def far_pieces(near, *first):
+    own, left, right = near
+    half = own.shape[0] // 2
+    halves = [after(a, *first) for a in (left[:half], right[half:])]
+    return [shift(halves[0], "x", 1), shift(halves[1], "x", -1)]
+
+
+def plan_of(far_count, row):
+    plan = []
+    for at in (0, 3 + far_count):
+        plan += [((at + d, None, row),) for d in range(3)]
+        plan.append(tuple((at + 3 + h, None, row) for h in range(far_count)))
+    return tuple(plan)
 
 
 def on_device(t2, keep, integrals):
     slots = integrals.shape[0]
     mx, mc = lax.axis_index("x"), lax.axis_index("c")
-    packed = pack(t2, keep, Y * Z, slots, GROUPS)
+    packed = pack(t2, keep, Y * Z, slots, [sum(g) for g in GROUPS])
     places = [((mx + d) % X) * C + c for c in (mc, 1 - mc) for d in (0, -1, 1, 2)]
     order = jnp.stack(places).astype(jnp.int32)
 
@@ -158,24 +181,20 @@
     for part in packed:
         part = after(part, *owns[-1:])
         owns.append(lax.all_to_all(part, ("y", "z"), split_axis=0, concat_axis=0, tiled=True))
-    results, earlier, last, before = [], [], [], []
-    for i, own in enumerate(owns):
-        own = after(own, *earlier)
-        left, right = shift(own, "x", 1), shift(own, "x", -1)
-        half = own.shape[0] // 2
-        halves = [after(a, *owns[i + 1 : i + 2]) for a in (left[:half], right[half:])]
-        far = [shift(halves[0], "x", 1), shift(halves[1], "x", -1)]
-        earlier = far if BY_FAR else [left, right]
-        mine = [[own], [left], [right], far]
-        near_held = [] if NEAR_FREE else last
-        theirs = [[swap(after(a, *near_held)) for a in piece] for piece in mine[:3]]
-        theirs.append([swap(after(a, *last)) for a in far])
-        blocks = product(mine + theirs, order, integrals)
-        sent = blocks.astype(jnp.float16)
-        last = [sent]
-        got, total = add_over_owners(after(sent, *before))
-        before = [got]
-        results.append(total)
+    results, before, last, near = [], [], [], []
+    for i, (own, group) in enumerate(zip(owns, GROUPS)):
+        near = near_pieces(after(own, *near))
+        far = far_pieces(near, *owns[i + 1 : i + 2])
+        near_across = [swap(a) for a in near]
+        arrays = near + far + near_across + [swap(after(a, *last)) for a in far]
+        row = 0
+        for rows in group:
+            arrays = [after(a, *last) for a in arrays]
+            blocks = product(arrays, plan_of(len(far), row), rows, order, integrals)
+            sent, got, total = at_once(blocks, *before)
+            before, last = [got], [sent]
+            results.append(as_rows(total, rows))
+            row += rows
     return (0.5 * jnp.concatenate(results, axis=0)).astype(jnp.bfloat16)
 
 

time: 177 us -> 173 us (0.977)
  local copies, waits for them, and re-layouts: 10.1 us -> 6.39 us
    all_to_all x2, starting transfers between devices: 13.5 us -> 9.27 us  [at_once(): lax.all_to_all(sent, ('y', 'z'), split_axis=0, concat_axis=0, tiled=True)]
    unnamed x12 -> x4, local copies, waits for them, and re-layouts: 5.94 us -> 2.2 us
    ppermute x18, starting transfers between devices: 12.1 us -> 14.5 us  [shift(): return lax.ppermute(a, axis, [(i, (i + by) % n) for i in range(n)])]
  transfers between devices with their start and end apart: 21 -> 21, of which waited for: 8 -> 9; matrix products, arithmetic and copies ran while one was open for 6% -> 6% of each run, Pallas kernels for 16% -> 16%
where the time goes in v4:
time: 173 us; the launch traced here: 172 us
  waiting for transfers between devices  73.9 us (43%)
  Pallas kernels  31.1 us (18%)
  starting transfers between devices  27.7 us (16%)
  blocking collectives  25 us (14%)
  other arithmetic  7.43 us (4%)
  local copies, waits for them, and re-layouts  6.39 us (4%)
    ppermute x18, waiting for transfers between devices, shift(): return lax.ppermute(a, axis, [(i, (i + by) % n) for i in range(n)])  45 us
    all_to_all x2, waiting for transfers between devices, at_once(): lax.all_to_all(sent, ('y', 'z'), split_axis=0, concat_axis=0, tiled=True)  28.9 us
    pallas_call x2, Pallas kernels, product(): pl.pallas_call(functools.partial(product_kernel, plan), out_shape=jax.Sha...  27.7 us
    all_to_all x1, blocking collectives, on_device(): lax.all_to_all(part, ('y', 'z'), split_axis=0, concat_axis=0, tiled=True)  25 us
    ppermute x18, starting transfers between devices, shift(): return lax.ppermute(a, axis, [(i, (i + by) % n) for i in range(n)])  14.5 us
    all_to_all x2, starting transfers between devices, at_once(): lax.all_to_all(sent, ('y', 'z'), split_axis=0, concat_axis=0, tiled=True)  9.27 us
    slice x4, local copies, waits for them, and re-layouts, far_pieces(): halves = [after(a, *first) for a in (left[:half], right[half:])]  4.07 us
    all_to_all x1, starting transfers between devices, on_device(): lax.all_to_all(part, ('y', 'z'), split_axis=0, concat_axis=0, tiled=True)  3.84 us
  transfers between devices with their start and end apart: 21, of which 9 were waited for; matrix products, arithmetic and copies ran while one was open for 6% of the time, Pallas kernels for 16%

profile of v4, /device:TPU:0, one launch (start us, length us, event | category | flops | bytes accessed | tf_op | source)
XLA Modules:
  0.0 171.7 jit_solution(1876892010776133783)
XLA Ops:
  0.0 3.5 %pack.1 = (bf16[16,4,64,128]{3,2,1,0:T(8,128)(2,1)}, bf16[16,4,64,128]{3,2,1,0:T(8,128)(2,1)}) custom-call(s32[40]{0:T(128)} %keep_ref.1, bf16[128,40,128]{2,1,0:T(8,128)(2,1)} %t2_ref.1), custom_call_target="tpu_custom_call" | custom-call | tf_op jit(solution)/shard_map/pack/pallas_call | solution.py:41
  3.5 25.0 %all_to_all.20.refs_0_ = bf16[16,4,64,128]{3,2,1,0:T(8,128)(2,1)S(1)} all-to-all(bf16[16,4,64,128]{3,2,1,0:T(8,128)(2,1)} %get-tuple-element.22), channel_id=1, replica_groups=mesh['x'=4,'c'=2,'y'=4,'z'=4] {'y','z'}, dimensions={0} | all-to-all | bytes 2097152 | tf_op jit(solution)/shard_map/all_to_all | solution.py:183
  28.5 1.5 collective-permute-start
  30.0 1.7 %collective-permute-start.1 = (bf16[16,4,64,128]{3,2,1,0:T(8,128)(2,1)S(1)}, bf16[16,4,64,128]{3,2,1,0:T(8,128)(2,1)}, u32[]{:S(2)}, u32[]{:S(2)}) collective-permute-start(bf16[16,4,64,128]{3,2,1,0:T(8,128)(2,1)S(1)} %all_to_all.20.refs_0_), channel_id=1, source_target_pairs={{0,96},{32,0},{64,32},{96,64},{1,97},{33,1},{65,33},{97,65},{2,98}... | collective-permute-start | bytes 3145736 | tf_op jit(solution)/shard_map/ppermute | solution.py:19
  31.7 3.8 %all-to-all-start.1 = ((bf16[16,4,64,128]{3,2,1,0:T(8,128)(2,1)}), bf16[16,4,64,128]{3,2,1,0:T(8,128)(2,1)S(1)}, u32[]{:S(2)}, u32[]{:S(2)}) async-start(bf16[16,4,64,128]{3,2,1,0:T(8,128)(2,1)} %get-tuple-element.24), calls=%async_computation.1 | async-start | bytes 2097152 | tf_op jit(solution)/shard_map/all_to_all | solution.py:183
  35.6 17.8 %collective-permute-done.refs_1_ = bf16[16,4,64,128]{3,2,1,0:T(8,128)(2,1)} collective-permute-done((bf16[16,4,64,128]{3,2,1,0:T(8,128)(2,1)S(1)}, bf16[16,4,64,128]{3,2,1,0:T(8,128)(2,1)}, u32[]{:S(2)}, u32[]{:S(2)}) %collective-permute-start) | collective-permute-done | bytes 1048608 | tf_op jit(solution)/shard_map/ppermute | solution.py:19
  53.4 1.9 %slice.32 = bf16[8,4,64,128]{3,2,1,0:T(8,128)(2,1)} slice(bf16[16,4,64,128]{3,2,1,0:T(8,128)(2,1)} %collective-permute-done.refs_1_), slice={[0:8], [0:4], [0:64], [0:128]} | slice | bytes 1048576 | tf_op jit(solution)/shard_map/slice | solution.py:161
  55.6 1.1 slice.33
  57.0 3.0 %collective-permute-start.3 = (bf16[8,4,64,128]{3,2,1,0:T(8,128)(2,1)S(1)}, bf16[8,4,64,128]{3,2,1,0:T(8,128)(2,1)}, u32[]{:S(2)}, u32[]{:S(2)}) collective-permute-start(bf16[8,4,64,128]{3,2,1,0:T(8,128)(2,1)S(1)} %slice.33), channel_id=1, source_target_pairs={{0,96},{32,0},{64,32},{96,64},{1,97},{33,1},{65,33},{97,65},{2,98}... | collective-permute-start | bytes 1572872 | tf_op jit(solution)/shard_map/ppermute | solution.py:19
  59.9 11.2 %collective-permute-done.2.refs_3_ = bf16[8,4,64,128]{3,2,1,0:T(8,128)(2,1)} collective-permute-done((bf16[8,4,64,128]{3,2,1,0:T(8,128)(2,1)}, bf16[8,4,64,128]{3,2,1,0:T(8,128)(2,1)}, u32[]{:S(2)}, u32[]{:S(2)}) %collective-permute-start.2) | collective-permute-done | bytes 524320 | tf_op jit(solution)/shard_map/ppermute | solution.py:19
  71.7 1.0 copy-done
  72.7 1.0 collective-permute-start.9
  73.7 2.7 %collective-permute-start.10 = (bf16[16,4,64,128]{3,2,1,0:T(8,128)(2,1)S(1)}, bf16[16,4,64,128]{3,2,1,0:T(8,128)(2,1)}, u32[]{:S(2)}, u32[]{:S(2)}) collective-permute-start(bf16[16,4,64,128]{3,2,1,0:T(8,128)(2,1)S(1)} %all-to-all-done.1.refs_0_), channel_id=1, source_target_pairs={{0,96},{32,0},{64,32},{96,64},{1,97},{33,1},{65,33},{97,65},{2,98}... | collective-permute-start | bytes 3145736 | tf_op jit(solution)/shard_map/ppermute | solution.py:19
  76.5 1.2 copy-done.1
  77.7 14.1 %product.2 = f32[16,2,264,128]{3,2,1,0:T(8,128)S(1)} custom-call(s32[8]{0:T(128)S(1)} %stack.35.order_ref, bf16[16,4,64,128]{3,2,1,0:T(8,128)(2,1)S(1)} %all_to_all.20.refs_0_, bf16[16,4,64,128]{3,2,1,0:T(8,128)(2,1)} %collective-permute-done.refs_1_, bf16[16,4,64,128]{3,2,1,0:T(8,128)(2,1)} %collective-permute-done.1.refs_2_, ...), custom_call_target="tpu_custom_call" | custom-call | flops 8589934592 | bytes 20971520 | tf_op jit(solution)/shard_map/product/pallas_call | solution.py:108
  91.8 1.6 convert_element_type.21
  93.4 4.4 %all-to-all-start.2 = ((f16[16,2,264,128]{3,2,1,0:T(8,128)(2,1)}), f16[16,2,264,128]{3,2,1,0:T(8,128)(2,1)}, u32[]{:S(2)}, u32[]{:S(2)}) async-start(f16[16,2,264,128]{3,2,1,0:T(8,128)(2,1)} %convert_element_type.21), calls=%async_computation.2 | async-start | bytes 4325376 | tf_op jit(solution)/shard_map/all_to_all | solution.py:137
  97.9 2.3 %collective-permute-done.9.refs_1_ = bf16[16,4,64,128]{3,2,1,0:T(8,128)(2,1)S(1)} collective-permute-done((bf16[16,4,64,128]{3,2,1,0:T(8,128)(2,1)S(1)}, bf16[16,4,64,128]{3,2,1,0:T(8,128)(2,1)S(1)}, u32[]{:S(2)}, u32[]{:S(2)}) %collective-permute-start.9) | collective-permute-done | bytes 1048608 | tf_op jit(solution)/shard_map/ppermute | solution.py:19
  100.4 1.1 slice.37
  101.5 3.2 %collective-permute-start.12 = (bf16[8,4,64,128]{3,2,1,0:T(8,128)(2,1)S(1)}, bf16[8,4,64,128]{3,2,1,0:T(8,128)(2,1)S(1)}, u32[]{:S(2)}, u32[]{:S(2)}) collective-permute-start(bf16[8,4,64,128]{3,2,1,0:T(8,128)(2,1)S(1)} %slice.37), channel_id=1, source_target_pairs={{0,96},{32,0},{64,32},{96,64},{1,97},{33,1},{65,33},{97,65},{2,98}... | collective-permute-start | bytes 1572872 | tf_op jit(solution)/shard_map/ppermute | solution.py:19
  105.2 10.1 %collective-permute-done.11.refs_3_ = bf16[8,4,64,128]{3,2,1,0:T(8,128)(2,1)S(1)} collective-permute-done((bf16[8,4,64,128]{3,2,1,0:T(8,128)(2,1)S(1)}, bf16[8,4,64,128]{3,2,1,0:T(8,128)(2,1)S(1)}, u32[]{:S(2)}, u32[]{:S(2)}) %collective-permute-start.11) | collective-permute-done | bytes 524320 | tf_op jit(solution)/shard_map/ppermute | solution.py:19
  115.3 1.3 collective-permute-done.12.refs_4_
  116.6 0.6 collective-permute-done.16.refs_8_
  117.2 1.3 collective-permute-done.17.refs_9_
  118.5 13.5 %product.3 = f32[16,2,264,128]{3,2,1,0:T(8,128)S(1)} custom-call(s32[8]{0:T(128)S(1)} %stack.35.order_ref, bf16[16,4,64,128]{3,2,1,0:T(8,128)(2,1)S(1)} %all-to-all-done.1.refs_0_, bf16[16,4,64,128]{3,2,1,0:T(8,128)(2,1)S(1)} %collective-permute-done.9.refs_1_, bf16[16,4,64,128]{3,2,1,0:T(8,128)(2,1)} %collective-permute-done.10.refs_2_, ...), custom_call_target="tpu_custom_call" | custom-call | flops 8589934592 | bytes 20971520 | tf_op jit(solution)/shard_map/product/pallas_call | solution.py:108
  132.0 1.7 convert_element_type.24
  133.7 4.8 %all-to-all-start.3 = ((f16[16,2,264,128]{3,2,1,0:T(8,128)(2,1)}), f16[16,2,264,128]{3,2,1,0:T(8,128)(2,1)S(1)}, u32[]{:S(2)}, u32[]{:S(2)}) async-start(f16[16,2,264,128]{3,2,1,0:T(8,128)(2,1)} %convert_element_type.24), calls=%async_computation.3 | async-start | bytes 4325376 | tf_op jit(solution)/shard_map/all_to_all | solution.py:137
  138.5 0.9 fusion.6
  139.4 2.1 %multiply_reduce_fusion.1 = f32[2,256,128]{2,1,0:T(8,128)S(1)} fusion(f16[16,2,264,128]{3,2,1,0:T(8,128)(2,1)} %all-to-all-done.2, f32[16,2,128]{2,1,0:T(2,128)S(1)} %bitcast.28), kind=kLoop, calls=%fused_computation.1 | loop fusion | flops 3080192 | bytes 2375680 | tf_op jit(solution)/shard_map/reduce_sum | solution.py:138
  141.5 28.9 %all-to-all-done.3 = f16[16,2,264,128]{3,2,1,0:T(8,128)(2,1)S(1)} async-done(((f16[16,2,264,128]{3,2,1,0:T(8,128)(2,1)}), f16[16,2,264,128]{3,2,1,0:T(8,128)(2,1)S(1)}, u32[]{:S(2)}, u32[]{:S(2)}) %all-to-all-start.3) | async-done | bytes 2162720 | tf_op jit(solution)/shard_map/all_to_all | solution.py:137
  170.5 0.4 multiply_reduce_fusion
  170.9 0.7 fusion
  (32 shorter events, 2.1 us)
Async XLA Ops:
  28.5 25.0 %collective-permute-start = (bf16[16,4,64,128]{3,2,1,0:T(8,128)(2,1)S(1)}, bf16[16,4,64,128]{3,2,1,0:T(8,128)(2,1)}, u32[]{:S(2)}, u32[]{:S(2)}) collective-permute-start(bf16[16,4,64,128]{3,2,1,0:T(8,128)(2,1)S(1)} %all_to_all.20.refs_0_), channel_id=1, source_target_pairs={{0,32},{32,64},{64,96},{96,0},{1,33},{33,65},{65,97},{97,1},{2,34}... | collective-permute-start | bytes 3145736 | tf_op jit(solution)/shard_map/ppermute | solution.py:19
  30.0 25.6 %collective-permute-start.1 = (bf16[16,4,64,128]{3,2,1,0:T(8,128)(2,1)S(1)}, bf16[16,4,64,128]{3,2,1,0:T(8,128)(2,1)}, u32[]{:S(2)}, u32[]{:S(2)}) collective-permute-start(bf16[16,4,64,128]{3,2,1,0:T(8,128)(2,1)S(1)} %all_to_all.20.refs_0_), channel_id=1, source_target_pairs={{0,96},{32,0},{64,32},{96,64},{1,97},{33,1},{65,33},{97,65},{2,98}... | collective-permute-start | bytes 3145736 | tf_op jit(solution)/shard_map/ppermute | solution.py:19
  31.7 23.6 %all-to-all-start.1 = ((bf16[16,4,64,128]{3,2,1,0:T(8,128)(2,1)}), bf16[16,4,64,128]{3,2,1,0:T(8,128)(2,1)S(1)}, u32[]{:S(2)}, u32[]{:S(2)}) async-start(bf16[16,4,64,128]{3,2,1,0:T(8,128)(2,1)} %get-tuple-element.24), calls=%async_computation.1 | async-start | bytes 2097152 | tf_op jit(solution)/shard_map/all_to_all | solution.py:183
  35.6 36.1 %collective-permute-start.4 = (bf16[16,4,64,128]{3,2,1,0:T(8,128)(2,1)S(1)}, bf16[16,4,64,128]{3,2,1,0:T(8,128)(2,1)S(1)}, u32[]{:S(2)}, u32[]{:S(2)}) collective-permute-start(bf16[16,4,64,128]{3,2,1,0:T(8,128)(2,1)S(1)} %all_to_all.20.refs_0_), channel_id=1, source_target_pairs={{0,16},{16,0},{1,17},{17,1},{2,18},{18,2},{3,19},{19,3},{4,20},{20... | collective-permute-start | bytes 3145736 | tf_op jit(solution)/shard_map/ppermute | solution.py:19
  53.4 20.3 %collective-permute-start.5 = (bf16[16,4,64,128]{3,2,1,0:T(8,128)(2,1)}, bf16[16,4,64,128]{3,2,1,0:T(8,128)(2,1)}, u32[]{:S(2)}, u32[]{:S(2)}) collective-permute-start(bf16[16,4,64,128]{3,2,1,0:T(8,128)(2,1)} %collective-permute-done.refs_1_), channel_id=1, source_target_pairs={{0,16},{16,0},{1,17},{17,1},{2,18},{18,2},{3,19},{19,3},{4,20},{20... | collective-permute-start | bytes 3145736 | tf_op jit(solution)/shard_map/ppermute | solution.py:19
  55.3 15.9 %collective-permute-start.2 = (bf16[8,4,64,128]{3,2,1,0:T(8,128)(2,1)}, bf16[8,4,64,128]{3,2,1,0:T(8,128)(2,1)}, u32[]{:S(2)}, u32[]{:S(2)}) collective-permute-start(bf16[8,4,64,128]{3,2,1,0:T(8,128)(2,1)} %slice.32), channel_id=1, source_target_pairs={{0,32},{32,64},{64,96},{96,0},{1,33},{33,65},{65,97},{97,1},{2,34}... | collective-permute-start | bytes 1572872 | tf_op jit(solution)/shard_map/ppermute | solution.py:19
  56.7 19.8 %collective-permute-start.6 = (bf16[16,4,64,128]{3,2,1,0:T(8,128)(2,1)}, bf16[16,4,64,128]{3,2,1,0:T(8,128)(2,1)}, u32[]{:S(2)}, u32[]{:S(2)}) collective-permute-start(bf16[16,4,64,128]{3,2,1,0:T(8,128)(2,1)} %collective-permute-done.1.refs_2_), channel_id=1, source_target_pairs={{0,16},{16,0},{1,17},{17,1},{2,18},{18,2},{3,19},{19,3},{4,20},{20... | collective-permute-start | bytes 3145736 | tf_op jit(solution)/shard_map/ppermute | solution.py:19
  57.0 14.6 %collective-permute-start.3 = (bf16[8,4,64,128]{3,2,1,0:T(8,128)(2,1)S(1)}, bf16[8,4,64,128]{3,2,1,0:T(8,128)(2,1)}, u32[]{:S(2)}, u32[]{:S(2)}) collective-permute-start(bf16[8,4,64,128]{3,2,1,0:T(8,128)(2,1)S(1)} %slice.33), channel_id=1, source_target_pairs={{0,96},{32,0},{64,32},{96,64},{1,97},{33,1},{65,33},{97,65},{2,98}... | collective-permute-start | bytes 1572872 | tf_op jit(solution)/shard_map/ppermute | solution.py:19
  71.2 5.3 %collective-permute-start.7 = (bf16[8,4,64,128]{3,2,1,0:T(8,128)(2,1)}, bf16[8,4,64,128]{3,2,1,0:T(8,128)(2,1)}, u32[]{:S(2)}, u32[]{:S(2)}) collective-permute-start(bf16[8,4,64,128]{3,2,1,0:T(8,128)(2,1)} %collective-permute-done.2.refs_3_), channel_id=1, source_target_pairs={{0,16},{16,0},{1,17},{17,1},{2,18},{18,2},{3,19},{19,3},{4,20},{20... | collective-permute-start | bytes 1572872 | tf_op jit(solution)/shard_map/ppermute | solution.py:19
  71.6 4.9 %collective-permute-start.8 = (bf16[8,4,64,128]{3,2,1,0:T(8,128)(2,1)}, bf16[8,4,64,128]{3,2,1,0:T(8,128)(2,1)}, u32[]{:S(2)}, u32[]{:S(2)}) collective-permute-start(bf16[8,4,64,128]{3,2,1,0:T(8,128)(2,1)} %collective-permute-done.3.refs_4_), channel_id=1, source_target_pairs={{0,16},{16,0},{1,17},{17,1},{2,18},{18,2},{3,19},{19,3},{4,20},{20... | collective-permute-start | bytes 1572872 | tf_op jit(solution)/shard_map/ppermute | solution.py:19
  71.7 1.0 copy-start
  72.7 27.5 %collective-permute-start.9 = (bf16[16,4,64,128]{3,2,1,0:T(8,128)(2,1)S(1)}, bf16[16,4,64,128]{3,2,1,0:T(8,128)(2,1)S(1)}, u32[]{:S(2)}, u32[]{:S(2)}) collective-permute-start(bf16[16,4,64,128]{3,2,1,0:T(8,128)(2,1)S(1)} %all-to-all-done.1.refs_0_), channel_id=1, source_target_pairs={{0,32},{32,64},{64,96},{96,0},{1,33},{33,65},{65,97},{97,1},{2,34}... | collective-permute-start | bytes 3145736 | tf_op jit(solution)/shard_map/ppermute | solution.py:19
  73.7 26.7 %collective-permute-start.10 = (bf16[16,4,64,128]{3,2,1,0:T(8,128)(2,1)S(1)}, bf16[16,4,64,128]{3,2,1,0:T(8,128)(2,1)}, u32[]{:S(2)}, u32[]{:S(2)}) collective-permute-start(bf16[16,4,64,128]{3,2,1,0:T(8,128)(2,1)S(1)} %all-to-all-done.1.refs_0_), channel_id=1, source_target_pairs={{0,96},{32,0},{64,32},{96,64},{1,97},{33,1},{65,33},{97,65},{2,98}... | collective-permute-start | bytes 3145736 | tf_op jit(solution)/shard_map/ppermute | solution.py:19
  76.5 1.2 copy-start.1
  93.4 40.2 %all-to-all-start.2 = ((f16[16,2,264,128]{3,2,1,0:T(8,128)(2,1)}), f16[16,2,264,128]{3,2,1,0:T(8,128)(2,1)}, u32[]{:S(2)}, u32[]{:S(2)}) async-start(f16[16,2,264,128]{3,2,1,0:T(8,128)(2,1)} %convert_element_type.21), calls=%async_computation.2 | async-start | bytes 4325376 | tf_op jit(solution)/shard_map/all_to_all | solution.py:137
  100.2 15.0 %collective-permute-start.11 = (bf16[8,4,64,128]{3,2,1,0:T(8,128)(2,1)S(1)}, bf16[8,4,64,128]{3,2,1,0:T(8,128)(2,1)S(1)}, u32[]{:S(2)}, u32[]{:S(2)}) collective-permute-start(bf16[8,4,64,128]{3,2,1,0:T(8,128)(2,1)S(1)} %slice.36), channel_id=1, source_target_pairs={{0,32},{32,64},{64,96},{96,0},{1,33},{33,65},{65,97},{97,1},{2,34}... | collective-permute-start | bytes 1572872 | tf_op jit(solution)/shard_map/ppermute | solution.py:19
  100.3 16.2 %collective-permute-start.13 = (bf16[16,4,64,128]{3,2,1,0:T(8,128)(2,1)S(1)}, bf16[16,4,64,128]{3,2,1,0:T(8,128)(2,1)S(1)}, u32[]{:S(2)}, u32[]{:S(2)}) collective-permute-start(bf16[16,4,64,128]{3,2,1,0:T(8,128)(2,1)S(1)} %all-to-all-done.1.refs_0_), channel_id=1, source_target_pairs={{0,16},{16,0},{1,17},{17,1},{2,18},{18,2},{3,19},{19,3},{4,20},{20... | collective-permute-start | bytes 3145736 | tf_op jit(solution)/shard_map/ppermute | solution.py:19
  101.5 15.0 %collective-permute-start.12 = (bf16[8,4,64,128]{3,2,1,0:T(8,128)(2,1)S(1)}, bf16[8,4,64,128]{3,2,1,0:T(8,128)(2,1)S(1)}, u32[]{:S(2)}, u32[]{:S(2)}) collective-permute-start(bf16[8,4,64,128]{3,2,1,0:T(8,128)(2,1)S(1)} %slice.37), channel_id=1, source_target_pairs={{0,96},{32,0},{64,32},{96,64},{1,97},{33,1},{65,33},{97,65},{2,98}... | collective-permute-start | bytes 1572872 | tf_op jit(solution)/shard_map/ppermute | solution.py:19
  104.7 13.8 %collective-permute-start.14 = (bf16[16,4,64,128]{3,2,1,0:T(8,128)(2,1)S(1)}, bf16[16,4,64,128]{3,2,1,0:T(8,128)(2,1)S(1)}, u32[]{:S(2)}, u32[]{:S(2)}) collective-permute-start(bf16[16,4,64,128]{3,2,1,0:T(8,128)(2,1)S(1)} %collective-permute-done.9.refs_1_), channel_id=1, source_target_pairs={{0,16},{16,0},{1,17},{17,1},{2,18},{18,2},{3,19},{19,3},{4,20},{20... | collective-permute-start | bytes 3145736 | tf_op jit(solution)/shard_map/ppermute | solution.py:19
  104.9 13.5 %collective-permute-start.15 = (bf16[16,4,64,128]{3,2,1,0:T(8,128)(2,1)}, bf16[16,4,64,128]{3,2,1,0:T(8,128)(2,1)S(1)}, u32[]{:S(2)}, u32[]{:S(2)}) collective-permute-start(bf16[16,4,64,128]{3,2,1,0:T(8,128)(2,1)} %collective-permute-done.10.refs_2_), channel_id=1, source_target_pairs={{0,16},{16,0},{1,17},{17,1},{2,18},{18,2},{3,19},{19,3},{4,20},{20... | collective-permute-start | bytes 3145736 | tf_op jit(solution)/shard_map/ppermute | solution.py:19
  115.3 1.9 %collective-permute-start.16 = (bf16[8,4,64,128]{3,2,1,0:T(8,128)(2,1)S(1)}, bf16[8,4,64,128]{3,2,1,0:T(8,128)(2,1)S(1)}, u32[]{:S(2)}, u32[]{:S(2)}) collective-permute-start(bf16[8,4,64,128]{3,2,1,0:T(8,128)(2,1)S(1)} %collective-permute-done.11.refs_3_), channel_id=1, source_target_pairs={{0,16},{16,0},{1,17},{17,1},{2,18},{18,2},{3,19},{19,3},{4,20},{20... | collective-permute-start | bytes 1572872 | tf_op jit(solution)/shard_map/ppermute | solution.py:19
  116.5 1.9 %collective-permute-start.17 = (bf16[8,4,64,128]{3,2,1,0:T(8,128)(2,1)S(1)}, bf16[8,4,64,128]{3,2,1,0:T(8,128)(2,1)S(1)}, u32[]{:S(2)}, u32[]{:S(2)}) collective-permute-start(bf16[8,4,64,128]{3,2,1,0:T(8,128)(2,1)S(1)} %collective-permute-done.12.refs_4_), channel_id=1, source_target_pairs={{0,16},{16,0},{1,17},{17,1},{2,18},{18,2},{3,19},{19,3},{4,20},{20... | collective-permute-start | bytes 1572872 | tf_op jit(solution)/shard_map/ppermute | solution.py:19
  133.7 36.7 %all-to-all-start.3 = ((f16[16,2,264,128]{3,2,1,0:T(8,128)(2,1)}), f16[16,2,264,128]{3,2,1,0:T(8,128)(2,1)S(1)}, u32[]{:S(2)}, u32[]{:S(2)}) async-start(f16[16,2,264,128]{3,2,1,0:T(8,128)(2,1)} %convert_element_type.24), calls=%async_computation.3 | async-start | bytes 4325376 | tf_op jit(solution)/shard_map/all_to_all | solution.py:137
